TPU v7x, 512 devices: a whole 4x8x8 slice. The times are simulated.
512 devices in a mesh: dp: 16 (over x, z_hi), section: 8 (over y), tensor: 4 (over z_lo, core).
Axes of the slice: x: 4, y: 8, z: 8 (z_hi: 4, z_lo: 2; z = z_hi * 2 + z_lo), core: 2. Of those that a mesh axis runs over, the one named last changes fastest.
Arguments:
- tokens: bfloat16 [2048, 8192], P('dp', 'tensor'), may hold values from -6 to 6
- owner_indices: int32 [2048, 1], P('dp'), may hold values from 0 to 15; in each aligned block of 64 rows (0 to 63, 64 to 127, ...) at most 5 rows name the same one
- local_adapter_index: int32 [2048], P('dp'), may hold values from 0 to 1
- gains: bfloat16 [8, 8192], P('section', 'tensor'), may hold values from 0.099609375 to 1.8984375
- adapter_down_weights: bfloat16 [8, 32, 64, 8192], P('section', 'dp', None, 'tensor'), may hold values from -0.0625 to 0.0625
- adapter_up_weights: bfloat16 [8, 32, 64, 8192], P('section', 'dp', None, 'tensor'), may hold values from -0.75 to 0.75
- cotangent: bfloat16 [2048, 8192], P('dp', 'tensor'), may hold values from -6 to 6
Outputs:
- grad_down: bfloat16 [8, 32, 64, 8192], P('section', 'dp', None, 'tensor')
- grad_up: bfloat16 [8, 32, 64, 8192], P('section', 'dp', None, 'tensor')
- norm_slopes: float32 [8, 2048], P('section', 'dp')
Inputs may be any that keep to these rules, and one draw needn't show every extreme that they name: `owner_indices`: in each aligned block of 64 rows (one micro-batch), no value appears in more than 5 rows.
All inputs are finite; a program needn't handle non-finite values.
Results may differ from a plain program's by a relative error of at most 0.02.
Values may be sent and summed in bfloat16 or wider, within the bound.
A program may use at most 64 MiB of HBM per device.

v0:
```python
import math

import jax
import jax.numpy as jnp
from jax import lax
from jax.sharding import PartitionSpec as P

MTOK = 64


eps = 1e-05
adapter_scale = 0.5


def shifted(x, axis, by):
    count = lax.axis_size(axis)
    pairs = [(i, i + by) for i in range(count) if 0 <= i + by < count]
    return lax.ppermute(x, axis, pairs)


def routing(owners, choose, block, groups, cap):
    start = block * MTOK
    own = lax.dynamic_slice_in_dim(owners, start, MTOK)
    which = lax.dynamic_slice_in_dim(choose, start, MTOK)
    onehot = (own[:, None] == jnp.arange(groups, dtype=jnp.int32)[None, :]).astype(jnp.int32)
    rank_in = jnp.sum((jnp.cumsum(onehot, 0) - onehot) * onehot, 1)
    place = own * cap + rank_in
    member = place[None, :] == jnp.arange(groups * cap, dtype=jnp.int32)[:, None]
    slot_sub = jnp.sum(jnp.where(member, which[None, :], 0), 1)
    return (member.astype(jnp.bfloat16), slot_sub.reshape(groups, cap))


def selector(flat_sub, count):
    return flat_sub[None, :] == jnp.arange(count, dtype=jnp.int32)[:, None]


def owner_rank(rows, flat_sub, down_matrix):
    part = jnp.einsum("sd,ard->asr", rows, down_matrix, preferred_element_type=jnp.float32)
    adapter_selection = selector(flat_sub, down_matrix.shape[0])
    partial_total_sum = jnp.sum(jnp.where(adapter_selection[:, :, None], part, 0.0), 0)
    return lax.psum(partial_total_sum, "tensor").astype(jnp.bfloat16)


def expand_from_rank(rank_latent, adapter_selection, weight):
    part = jnp.einsum("sr,ard->asd", rank_latent, weight, preferred_element_type=jnp.float32)
    return jnp.sum(jnp.where(adapter_selection[:, :, None], part, 0.0), 0)


def on_device(
    tokens,
    owner_indices,
    local_adapter_index,
    gains,
    adapter_down_weights,
    adapter_up_weights,
    cotangent,
):
    groups = lax.axis_size("dp")
    sections = lax.axis_size("section")
    section = lax.axis_index("section")
    shard_width = tokens.shape[1]
    width = shard_width * lax.axis_size("tensor")
    micro = tokens.shape[0] // MTOK
    cap = 5 * MTOK // (4 * groups)
    slots = groups * cap
    steps = micro + sections - 1
    gain = gains[0].astype(jnp.float32)
    down_matrix = adapter_down_weights[0]
    up_matrix = adapter_up_weights[0]
    owners = owner_indices[:, 0]
    adapters = down_matrix.shape[0]

    def forward_step(inbox, step):
        block = step - section
        live = (block >= 0) & (block < micro)
        clipped = jnp.clip(block, 0, micro - 1)
        own_rows = lax.dynamic_slice_in_dim(tokens, clipped * MTOK, MTOK, 0)
        current = jnp.where(section == 0, own_rows, inbox)
        wide = current.astype(jnp.float32)
        total = lax.psum(jnp.sum(wide * wide, 1), "tensor")
        scale_rows = lax.rsqrt(total / width + eps)
        normed = (wide * scale_rows[:, None] * gain).astype(jnp.bfloat16)
        normed = jnp.where(live, normed, jnp.zeros_like(normed))
        member, slot_sub = routing(owners, local_adapter_index, clipped, groups, cap)
        outgoing = jnp.dot(member, normed, preferred_element_type=jnp.float32).astype(jnp.bfloat16)
        arrived, arrived_sub = (
            lax.all_to_all(
                outgoing.reshape(groups, cap, shard_width),
                "dp",
                split_axis=0,
                concat_axis=0,
                tiled=True,
            ),
            lax.all_to_all(slot_sub, "dp", split_axis=0, concat_axis=0, tiled=True),
        )
        rows = arrived.reshape(slots, shard_width)
        flat_sub = arrived_sub.reshape(slots)
        rank_latent = owner_rank(rows, flat_sub, down_matrix)
        adapter_selection = selector(flat_sub, adapters)
        adapter_branch = (
            adapter_scale * expand_from_rank(rank_latent, adapter_selection, up_matrix)
        ).astype(jnp.bfloat16)
        returned = lax.all_to_all(
            adapter_branch.reshape(groups, cap, shard_width),
            "dp",
            split_axis=0,
            concat_axis=0,
            tiled=True,
        )
        added = jnp.einsum(
            "st,sd->td",
            member,
            returned.reshape(slots, shard_width),
            preferred_element_type=jnp.float32,
        )
        result = (wide + added).astype(jnp.bfloat16)
        inbox_next = shifted(result, "section", 1)
        saved = (current, scale_rows, rows, flat_sub, rank_latent)
        return (inbox_next, saved)

    start_box = jnp.zeros((MTOK, shard_width), jnp.bfloat16)
    final_box, saved = lax.scan(forward_step, start_box, jnp.arange(steps, dtype=jnp.int32))

    def backward_step(carry, step):
        inbox, acc_down, up_accumulator = carry
        block = step - (sections - 1 - section)
        live = (block >= 0) & (block < micro)
        clipped = jnp.clip(block, 0, micro - 1)
        own_rows = lax.dynamic_slice_in_dim(cotangent, clipped * MTOK, MTOK, 0)
        incoming = jnp.where(section == sections - 1, own_rows, inbox)
        incoming = jnp.where(live, incoming, jnp.zeros_like(incoming))
        index = clipped + section
        current = lax.dynamic_index_in_dim(saved[0], index, 0, keepdims=False)
        scale_rows = lax.dynamic_index_in_dim(saved[1], index, 0, keepdims=False)
        wide = current.astype(jnp.float32)
        member, slot_sub = routing(owners, local_adapter_index, clipped, groups, cap)
        outgoing = jnp.dot(member, incoming, preferred_element_type=jnp.float32).astype(
            jnp.bfloat16
        )
        rows = lax.dynamic_index_in_dim(saved[2], index, 0, keepdims=False)
        flat_sub = lax.dynamic_index_in_dim(saved[3], index, 0, keepdims=False)
        rank_latent = lax.dynamic_index_in_dim(saved[4], index, 0, keepdims=False)
        arrived = lax.all_to_all(
            outgoing.reshape(groups, cap, shard_width),
            "dp",
            split_axis=0,
            concat_axis=0,
            tiled=True,
        )
        cotangent_rows = arrived.reshape(slots, shard_width)
        adapter_selection = selector(flat_sub, adapters)
        masked_latent = jnp.where(
            adapter_selection[:, :, None], rank_latent[None], jnp.zeros_like(rank_latent)[None]
        )
        up_accumulator = up_accumulator + adapter_scale * jnp.einsum(
            "asr,sd->ard", masked_latent, cotangent_rows, preferred_element_type=jnp.float32
        )
        part = jnp.einsum(
            "sd,ard->asr", cotangent_rows, up_matrix, preferred_element_type=jnp.float32
        )
        partial_total_sum = adapter_scale * jnp.sum(
            jnp.where(adapter_selection[:, :, None], part, 0.0), 0
        )
        rank_gradient = lax.psum(partial_total_sum, "tensor").astype(jnp.bfloat16)
        masked_grad = jnp.where(
            adapter_selection[:, :, None], rank_gradient[None], jnp.zeros_like(rank_gradient)[None]
        )
        acc_down = acc_down + jnp.einsum(
            "asr,sd->ard", masked_grad, rows, preferred_element_type=jnp.float32
        )
        normalized_gradient = expand_from_rank(
            rank_gradient, adapter_selection, down_matrix
        ).astype(jnp.bfloat16)
        returned = lax.all_to_all(
            normalized_gradient.reshape(groups, cap, shard_width),
            "dp",
            split_axis=0,
            concat_axis=0,
            tiled=True,
        )
        spread = (
            jnp.einsum(
                "st,sd->td",
                member,
                returned.reshape(slots, shard_width),
                preferred_element_type=jnp.float32,
            )
            * gain
        )
        product = lax.psum(jnp.sum(spread * wide, 1), "tensor") / width
        slope = product * scale_rows * math.sqrt(width)
        result = (
            incoming.astype(jnp.float32)
            + scale_rows[:, None] * spread
            - (scale_rows**3 * product)[:, None] * wide
        ).astype(jnp.bfloat16)
        inbox_next = shifted(result, "section", -1)
        return ((inbox_next, acc_down, up_accumulator), slope)

    empty = jnp.zeros(down_matrix.shape, jnp.float32)
    start_carry = (jnp.zeros((MTOK, shard_width), jnp.bfloat16), empty, empty)
    final_carry, slope_steps = lax.scan(
        backward_step, start_carry, jnp.arange(steps, dtype=jnp.int32)
    )
    grad_down = final_carry[1].astype(jnp.bfloat16)[None]
    grad_up = final_carry[2].astype(jnp.bfloat16)[None]
    first_live = sections - 1 - section
    live_slopes = lax.dynamic_slice_in_dim(slope_steps, first_live, micro, 0)
    norm_slopes = live_slopes.reshape(1, micro * MTOK)
    return (grad_down, grad_up, norm_slopes)


def solution(mesh):
    return jax.shard_map(
        on_device,
        mesh=mesh,
        in_specs=(
            P("dp", "tensor"),
            P("dp", None),
            P("dp"),
            P("section", "tensor"),
            P("section", "dp", None, "tensor"),
            P("section", "dp", None, "tensor"),
            P("dp", "tensor"),
        ),
        out_specs=(
            P("section", "dp", None, "tensor"),
            P("section", "dp", None, "tensor"),
            P("section", "dp"),
        ),
        check_vma=False,
    )
```

profile of v0, /device:TPU:1, one launch (start us, length us, event | category | flops | bytes accessed | tf_op | source)
XLA Modules:
  0.0 1576.0 jit_solution(2222565465980676570)
XLA Ops:
  1.4 821.2 %while.39 = (s32[]{:T(128)}, bf16[64,2048]{1,0:T(8,128)(2,1)S(1)}, bf16[9,64,2048]{2,1,0:T(8,128)(2,1)}, f32[9,64]{1,0:T(8,128)S(1)}, bf16[9,80,2048]{2,1,0:T(8,...) while((s32[]{:T(128)}, bf16[64,2048]{1,0:T(8,128)(2,1)S(1)}, ...), condition=%wide.region_9.10_spmd, body=%wide.region_0.9_spmd.sunk | while | flops 128503072 | bytes 17835340 | solution.py:122
  72.8 15.4 all-to-all-done.2
  162.3 15.4 all-to-all-done.2
  252.6 15.3 all-to-all-done.2
  343.0 15.4 all-to-all-done.2
  433.4 15.4 all-to-all-done.2
  523.8 15.4 all-to-all-done.2
  615.0 15.4 all-to-all-done.2
  706.5 15.4 all-to-all-done.2
  798.1 15.4 all-to-all-done.2
  822.6 751.7 %while.40 = (s32[]{:T(128)}, bf16[64,2048]{1,0:T(8,128)(2,1)S(1)}, f32[2,64,2048]{2,1,0:T(8,128)S(1)}, f32[2,64,2048]{2,1,0:T(8,128)S(1)}, f32[9,64]{1,0:T(8,128...) while((s32[]{:T(128)}, bf16[64,2048]{1,0:T(8,128)(2,1)S(1)}, ...), condition=%wide.region_18.19_spmd.clone, body=%wide.region_10.18_spmd.clone.sunk | while | flops 213776048 | bytes 20886368 | solution.py:202
  844.5 20.1 %psum.40 = bf16[80,64]{0,1:T(8,128)(2,1)S(1)} all-reduce(f32[80,64]{0,1:T(8,128)S(1)} %broadcast_multiply_fusion.2), channel_id=1, replica_groups=mesh['dp'=16,'section'=8,'tensor'=4] {'tensor'}, use_global_device_ids=true, to_apply=%region_14.14 | all-reduce | flops 5120 | bytes 30720 | tf_op jit(solution)/shard_map/while/body/eval_jaxpr/psum | solution.py:164
  871.7 15.3 all-to-all-done.4
  918.8 17.2 %all-to-all-done.3 = bf16[16,5,2048]{2,1,0:T(8,128)(2,1)S(1)} async-done(((bf16[16,5,2048]{2,1,0:T(8,128)(2,1)}), bf16[16,5,2048]{2,1,0:T(8,128)(2,1)S(1)}, u32[]{:S(2)}, u32[]{:S(2)}) %all-to-all-start.3) | async-done | bytes 327712 | tf_op jit(solution)/shard_map/while/body/eval_jaxpr/all_to_all | solution.py:143
  955.9 16.5 %all-to-all-done.4 = bf16[16,5,2048]{2,1,0:T(8,128)(2,1)S(1)} async-done(((bf16[16,5,2048]{2,1,0:T(8,128)(2,1)}), bf16[16,5,2048]{2,1,0:T(8,128)(2,1)S(1)}, u32[]{:S(2)}, u32[]{:S(2)}) %all-to-all-start.4) | async-done | bytes 327712 | tf_op jit(solution)/shard_map/while/body/eval_jaxpr/all_to_all | solution.py:174
  1002.1 15.7 all-to-all-done.3
  1086.6 17.1 %all-to-all-done.3 = bf16[16,5,2048]{2,1,0:T(8,128)(2,1)S(1)} async-done(((bf16[16,5,2048]{2,1,0:T(8,128)(2,1)}), bf16[16,5,2048]{2,1,0:T(8,128)(2,1)S(1)}, u32[]{:S(2)}, u32[]{:S(2)}) %all-to-all-start.3) | async-done | bytes 327712 | tf_op jit(solution)/shard_map/while/body/eval_jaxpr/all_to_all | solution.py:143
  1170.1 15.7 all-to-all-done.3
  1252.9 16.5 %all-to-all-done.3 = bf16[16,5,2048]{2,1,0:T(8,128)(2,1)S(1)} async-done(((bf16[16,5,2048]{2,1,0:T(8,128)(2,1)}), bf16[16,5,2048]{2,1,0:T(8,128)(2,1)S(1)}, u32[]{:S(2)}, u32[]{:S(2)}) %all-to-all-start.3) | async-done | bytes 327712 | tf_op jit(solution)/shard_map/while/body/eval_jaxpr/all_to_all | solution.py:143
  1289.9 15.9 %all-to-all-done.4 = bf16[16,5,2048]{2,1,0:T(8,128)(2,1)S(1)} async-done(((bf16[16,5,2048]{2,1,0:T(8,128)(2,1)}), bf16[16,5,2048]{2,1,0:T(8,128)(2,1)S(1)}, u32[]{:S(2)}, u32[]{:S(2)}) %all-to-all-start.4) | async-done | bytes 327712 | tf_op jit(solution)/shard_map/while/body/eval_jaxpr/all_to_all | solution.py:174
  1335.0 16.1 %all-to-all-done.3 = bf16[16,5,2048]{2,1,0:T(8,128)(2,1)S(1)} async-done(((bf16[16,5,2048]{2,1,0:T(8,128)(2,1)}), bf16[16,5,2048]{2,1,0:T(8,128)(2,1)S(1)}, u32[]{:S(2)}, u32[]{:S(2)}) %all-to-all-start.3) | async-done | bytes 327712 | tf_op jit(solution)/shard_map/while/body/eval_jaxpr/all_to_all | solution.py:143
  1418.0 17.3 %all-to-all-done.3 = bf16[16,5,2048]{2,1,0:T(8,128)(2,1)S(1)} async-done(((bf16[16,5,2048]{2,1,0:T(8,128)(2,1)}), bf16[16,5,2048]{2,1,0:T(8,128)(2,1)S(1)}, u32[]{:S(2)}, u32[]{:S(2)}) %all-to-all-start.3) | async-done | bytes 327712 | tf_op jit(solution)/shard_map/while/body/eval_jaxpr/all_to_all | solution.py:143
  1455.0 15.1 all-to-all-done.4
  1500.4 15.6 all-to-all-done.3
  (741 shorter events, 1208.5 us)
Async XLA Ops:
  6.0 22.7 %all-to-all-start = ((s32[16,1,5]{2,1,0:T(1,128)}), s32[16,1,5]{2,1,0:T(1,128)S(1)}, u32[]{:S(2)}, u32[]{:S(2)}) async-start(s32[16,1,5]{2,1,0:T(1,128)} %bitcast.113), calls=%async_computation | async-start | bytes 16384 | tf_op jit(solution)/shard_map/while/body/eval_jaxpr/all_to_all | solution.py:94
  28.7 24.7 %all-to-all-start.1 = ((bf16[16,5,2048]{2,1,0:T(8,128)(2,1)}), bf16[16,5,2048]{2,1,0:T(8,128)(2,1)S(1)}, u32[]{:S(2)}, u32[]{:S(2)}) async-start(bf16[16,5,2048]{2,1,0:T(8,128)(2,1)} %reshape.146), calls=%async_computation.1 | async-start | bytes 1048576 | tf_op jit(solution)/shard_map/while/body/eval_jaxpr/all_to_all | solution.py:87
  118.2 24.8 %all-to-all-start.1 = ((bf16[16,5,2048]{2,1,0:T(8,128)(2,1)}), bf16[16,5,2048]{2,1,0:T(8,128)(2,1)S(1)}, u32[]{:S(2)}, u32[]{:S(2)}) async-start(bf16[16,5,2048]{2,1,0:T(8,128)(2,1)} %reshape.146), calls=%async_computation.1 | async-start | bytes 1048576 | tf_op jit(solution)/shard_map/while/body/eval_jaxpr/all_to_all | solution.py:87
  208.5 24.9 %all-to-all-start.1 = ((bf16[16,5,2048]{2,1,0:T(8,128)(2,1)}), bf16[16,5,2048]{2,1,0:T(8,128)(2,1)S(1)}, u32[]{:S(2)}, u32[]{:S(2)}) async-start(bf16[16,5,2048]{2,1,0:T(8,128)(2,1)} %reshape.146), calls=%async_computation.1 | async-start | bytes 1048576 | tf_op jit(solution)/shard_map/while/body/eval_jaxpr/all_to_all | solution.py:87
  298.9 24.8 %all-to-all-start.1 = ((bf16[16,5,2048]{2,1,0:T(8,128)(2,1)}), bf16[16,5,2048]{2,1,0:T(8,128)(2,1)S(1)}, u32[]{:S(2)}, u32[]{:S(2)}) async-start(bf16[16,5,2048]{2,1,0:T(8,128)(2,1)} %reshape.146), calls=%async_computation.1 | async-start | bytes 1048576 | tf_op jit(solution)/shard_map/while/body/eval_jaxpr/all_to_all | solution.py:87
  389.3 24.8 %all-to-all-start.1 = ((bf16[16,5,2048]{2,1,0:T(8,128)(2,1)}), bf16[16,5,2048]{2,1,0:T(8,128)(2,1)S(1)}, u32[]{:S(2)}, u32[]{:S(2)}) async-start(bf16[16,5,2048]{2,1,0:T(8,128)(2,1)} %reshape.146), calls=%async_computation.1 | async-start | bytes 1048576 | tf_op jit(solution)/shard_map/while/body/eval_jaxpr/all_to_all | solution.py:87
  479.7 24.8 %all-to-all-start.1 = ((bf16[16,5,2048]{2,1,0:T(8,128)(2,1)}), bf16[16,5,2048]{2,1,0:T(8,128)(2,1)S(1)}, u32[]{:S(2)}, u32[]{:S(2)}) async-start(bf16[16,5,2048]{2,1,0:T(8,128)(2,1)} %reshape.146), calls=%async_computation.1 | async-start | bytes 1048576 | tf_op jit(solution)/shard_map/while/body/eval_jaxpr/all_to_all | solution.py:87
  570.9 24.8 %all-to-all-start.1 = ((bf16[16,5,2048]{2,1,0:T(8,128)(2,1)}), bf16[16,5,2048]{2,1,0:T(8,128)(2,1)S(1)}, u32[]{:S(2)}, u32[]{:S(2)}) async-start(bf16[16,5,2048]{2,1,0:T(8,128)(2,1)} %reshape.146), calls=%async_computation.1 | async-start | bytes 1048576 | tf_op jit(solution)/shard_map/while/body/eval_jaxpr/all_to_all | solution.py:87
  662.5 24.9 %all-to-all-start.1 = ((bf16[16,5,2048]{2,1,0:T(8,128)(2,1)}), bf16[16,5,2048]{2,1,0:T(8,128)(2,1)S(1)}, u32[]{:S(2)}, u32[]{:S(2)}) async-start(bf16[16,5,2048]{2,1,0:T(8,128)(2,1)} %reshape.146), calls=%async_computation.1 | async-start | bytes 1048576 | tf_op jit(solution)/shard_map/while/body/eval_jaxpr/all_to_all | solution.py:87
  754.1 24.9 %all-to-all-start.1 = ((bf16[16,5,2048]{2,1,0:T(8,128)(2,1)}), bf16[16,5,2048]{2,1,0:T(8,128)(2,1)S(1)}, u32[]{:S(2)}, u32[]{:S(2)}) async-start(bf16[16,5,2048]{2,1,0:T(8,128)(2,1)} %reshape.146), calls=%async_computation.1 | async-start | bytes 1048576 | tf_op jit(solution)/shard_map/while/body/eval_jaxpr/all_to_all | solution.py:87
  866.9 20.0 %all-to-all-start.4 = ((bf16[16,5,2048]{2,1,0:T(8,128)(2,1)}), bf16[16,5,2048]{2,1,0:T(8,128)(2,1)S(1)}, u32[]{:S(2)}, u32[]{:S(2)}) async-start(bf16[16,5,2048]{2,1,0:T(8,128)(2,1)} %convert_element_type.161), calls=%async_computation.4 | async-start | bytes 1048576 | tf_op jit(solution)/shard_map/while/body/eval_jaxpr/all_to_all | solution.py:174
  915.2 20.8 %all-to-all-start.3 = ((bf16[16,5,2048]{2,1,0:T(8,128)(2,1)}), bf16[16,5,2048]{2,1,0:T(8,128)(2,1)S(1)}, u32[]{:S(2)}, u32[]{:S(2)}) async-start(bf16[16,5,2048]{2,1,0:T(8,128)(2,1)} %reshape.149), calls=%async_computation.3 | async-start | bytes 1048576 | tf_op jit(solution)/shard_map/while/body/eval_jaxpr/all_to_all | solution.py:143
  951.2 21.2 %all-to-all-start.4 = ((bf16[16,5,2048]{2,1,0:T(8,128)(2,1)}), bf16[16,5,2048]{2,1,0:T(8,128)(2,1)S(1)}, u32[]{:S(2)}, u32[]{:S(2)}) async-start(bf16[16,5,2048]{2,1,0:T(8,128)(2,1)} %convert_element_type.161), calls=%async_computation.4 | async-start | bytes 1048576 | tf_op jit(solution)/shard_map/while/body/eval_jaxpr/all_to_all | solution.py:174
  1034.6 19.6 %all-to-all-start.4 = ((bf16[16,5,2048]{2,1,0:T(8,128)(2,1)}), bf16[16,5,2048]{2,1,0:T(8,128)(2,1)S(1)}, u32[]{:S(2)}, u32[]{:S(2)}) async-start(bf16[16,5,2048]{2,1,0:T(8,128)(2,1)} %convert_element_type.161), calls=%async_computation.4 | async-start | bytes 1048576 | tf_op jit(solution)/shard_map/while/body/eval_jaxpr/all_to_all | solution.py:174
  1083.0 20.8 %all-to-all-start.3 = ((bf16[16,5,2048]{2,1,0:T(8,128)(2,1)}), bf16[16,5,2048]{2,1,0:T(8,128)(2,1)S(1)}, u32[]{:S(2)}, u32[]{:S(2)}) async-start(bf16[16,5,2048]{2,1,0:T(8,128)(2,1)} %reshape.149), calls=%async_computation.3 | async-start | bytes 1048576 | tf_op jit(solution)/shard_map/while/body/eval_jaxpr/all_to_all | solution.py:143
  1118.8 19.6 %all-to-all-start.4 = ((bf16[16,5,2048]{2,1,0:T(8,128)(2,1)}), bf16[16,5,2048]{2,1,0:T(8,128)(2,1)S(1)}, u32[]{:S(2)}, u32[]{:S(2)}) async-start(bf16[16,5,2048]{2,1,0:T(8,128)(2,1)} %convert_element_type.161), calls=%async_computation.4 | async-start | bytes 1048576 | tf_op jit(solution)/shard_map/while/body/eval_jaxpr/all_to_all | solution.py:174
  1202.6 19.6 %all-to-all-start.4 = ((bf16[16,5,2048]{2,1,0:T(8,128)(2,1)}), bf16[16,5,2048]{2,1,0:T(8,128)(2,1)S(1)}, u32[]{:S(2)}, u32[]{:S(2)}) async-start(bf16[16,5,2048]{2,1,0:T(8,128)(2,1)} %convert_element_type.161), calls=%async_computation.4 | async-start | bytes 1048576 | tf_op jit(solution)/shard_map/while/body/eval_jaxpr/all_to_all | solution.py:174
  1249.3 20.1 %all-to-all-start.3 = ((bf16[16,5,2048]{2,1,0:T(8,128)(2,1)}), bf16[16,5,2048]{2,1,0:T(8,128)(2,1)S(1)}, u32[]{:S(2)}, u32[]{:S(2)}) async-start(bf16[16,5,2048]{2,1,0:T(8,128)(2,1)} %reshape.149), calls=%async_computation.3 | async-start | bytes 1048576 | tf_op jit(solution)/shard_map/while/body/eval_jaxpr/all_to_all | solution.py:143
  1285.2 20.7 %all-to-all-start.4 = ((bf16[16,5,2048]{2,1,0:T(8,128)(2,1)}), bf16[16,5,2048]{2,1,0:T(8,128)(2,1)S(1)}, u32[]{:S(2)}, u32[]{:S(2)}) async-start(bf16[16,5,2048]{2,1,0:T(8,128)(2,1)} %convert_element_type.161), calls=%async_computation.4 | async-start | bytes 1048576 | tf_op jit(solution)/shard_map/while/body/eval_jaxpr/all_to_all | solution.py:174
  1331.4 19.7 %all-to-all-start.3 = ((bf16[16,5,2048]{2,1,0:T(8,128)(2,1)}), bf16[16,5,2048]{2,1,0:T(8,128)(2,1)S(1)}, u32[]{:S(2)}, u32[]{:S(2)}) async-start(bf16[16,5,2048]{2,1,0:T(8,128)(2,1)} %reshape.149), calls=%async_computation.3 | async-start | bytes 1048576 | tf_op jit(solution)/shard_map/while/body/eval_jaxpr/all_to_all | solution.py:143
  1367.3 19.5 %all-to-all-start.4 = ((bf16[16,5,2048]{2,1,0:T(8,128)(2,1)}), bf16[16,5,2048]{2,1,0:T(8,128)(2,1)S(1)}, u32[]{:S(2)}, u32[]{:S(2)}) async-start(bf16[16,5,2048]{2,1,0:T(8,128)(2,1)} %convert_element_type.161), calls=%async_computation.4 | async-start | bytes 1048576 | tf_op jit(solution)/shard_map/while/body/eval_jaxpr/all_to_all | solution.py:174
  1414.4 21.0 %all-to-all-start.3 = ((bf16[16,5,2048]{2,1,0:T(8,128)(2,1)}), bf16[16,5,2048]{2,1,0:T(8,128)(2,1)S(1)}, u32[]{:S(2)}, u32[]{:S(2)}) async-start(bf16[16,5,2048]{2,1,0:T(8,128)(2,1)} %reshape.149), calls=%async_computation.3 | async-start | bytes 1048576 | tf_op jit(solution)/shard_map/while/body/eval_jaxpr/all_to_all | solution.py:143
  1450.2 19.8 %all-to-all-start.4 = ((bf16[16,5,2048]{2,1,0:T(8,128)(2,1)}), bf16[16,5,2048]{2,1,0:T(8,128)(2,1)S(1)}, u32[]{:S(2)}, u32[]{:S(2)}) async-start(bf16[16,5,2048]{2,1,0:T(8,128)(2,1)} %convert_element_type.161), calls=%async_computation.4 | async-start | bytes 1048576 | tf_op jit(solution)/shard_map/while/body/eval_jaxpr/all_to_all | solution.py:174
  1532.9 19.6 %all-to-all-start.4 = ((bf16[16,5,2048]{2,1,0:T(8,128)(2,1)}), bf16[16,5,2048]{2,1,0:T(8,128)(2,1)S(1)}, u32[]{:S(2)}, u32[]{:S(2)}) async-start(bf16[16,5,2048]{2,1,0:T(8,128)(2,1)} %convert_element_type.161), calls=%async_computation.4 | async-start | bytes 1048576 | tf_op jit(solution)/shard_map/while/body/eval_jaxpr/all_to_all | solution.py:174
  (84 other events, 1888.5 us)
where the time goes:
time: 1590 us; the launch traced here: 1580 us
  waiting for transfers between devices  633 us (40%)
  blocking collectives  427 us (27%)
  starting transfers between devices  274 us (17%)
  local copies, waits for them, and re-layouts  103 us (6%)
  matrix products  65.6 us (4%)
  other arithmetic  57.7 us (4%)
    all_to_all x9, waiting for transfers between devices, backward_step(): lax.all_to_all(outgoing.reshape(groups, cap, shard_width), 'dp', split_ax...  144 us
    all_to_all x9, waiting for transfers between devices, forward_step(): lax.all_to_all(adapter_branch.reshape(groups, cap, shard_width), 'dp', sp...  138 us
    all_to_all x9, waiting for transfers between devices, backward_step(): lax.all_to_all(normalized_gradient.reshape(groups, cap, shard_width), 'dp...  137 us
    all_to_all x9, waiting for transfers between devices, forward_step(): lax.all_to_all(outgoing.reshape(groups, cap, shard_width), 'dp', split_ax...  128 us
    psum x9, blocking collectives, backward_step(): rank_gradient = lax.psum(partial_total_sum, 'tensor').astype(jnp.bfloat16)  125 us
    psum x9, blocking collectives, owner_rank(): return lax.psum(partial_total_sum, 'tensor').astype(jnp.bfloat16)  124 us
    psum x9, blocking collectives, forward_step(): total = lax.psum(jnp.sum(wide * wide, 1), 'tensor')  100 us
    ppermute x18, waiting for transfers between devices, shifted(): return lax.ppermute(x, axis, pairs)  87 us
  transfers between devices with their start and end apart: 63, of which 54 were waited for; matrix products, arithmetic and copies ran while one was open for 5% of the time, Pallas kernels for 0%

commit v1 on v0

v1 whole, which is shorter than its diff:
```python
import functools
import math

import jax
import jax.numpy as jnp
import numpy as np
from jax import lax
from jax.experimental import pallas as pl
from jax.experimental.pallas import tpu as pltpu
from jax.sharding import PartitionSpec as P

MTOK = 64
LANES = 128
TILE = 16
EPS = 1e-05
SCALE = 0.5
MESH = pl.DeviceIdType.MESH


def round_up(value, unit):
    return -(-value // unit) * unit


def matmul(a, b, contract):
    return lax.dot_general(a, b, (contract, ((), ())), preferred_element_type=jnp.float32)


def drain(ref, sem):
    pltpu.make_async_copy(ref, ref, sem).wait()


def peers(axis):
    count, me = lax.axis_size(axis), lax.axis_index(axis)
    return [(o - 1, lax.rem(me + o, count)) for o in range(1, count)]


def kernel(
    cap,
    own_col,
    own_row,
    choose_row,
    gains,
    down,
    compact,
    tokens,
    cotangent,
    up,
    grad_down,
    grad_up,
    slopes,
    sendbuf,
    recvbuf,
    tokv,
    cotv,
    down_scaled,
    w_down,
    w_up,
    p1,
    f1,
    p2,
    f2,
    q1,
    h1,
    q2,
    h2,
    xs,
    zs,
    rs,
    cur,
    first_cot,
    mask,
    back_d,
    back_u,
    slope_rows,
    loc_sem,
    tok_s,
    tok_r,
    wd_s,
    wu_s,
    wd_r,
    wu_r,
    ss1,
    rs1,
    ss2,
    rs2,
    gd_s,
    gu_s,
    gd_r,
    gu_r,
    sl_s,
    sl_r,
):
    dp = lax.axis_index("dp")
    section = lax.axis_index("section")
    groups = lax.axis_size("dp")
    layers = lax.axis_size("section")
    count = tokens.shape[0]
    fw = tokv.shape[1]
    width = tokens.shape[1] * lax.axis_size("tensor")
    spad = sendbuf.shape[1]
    slots = xs.shape[1]
    half = slots // 2

    barrier = pltpu.get_barrier_semaphore()
    greeted = 0
    for axis in ("tensor", "section", "dp"):
        for _, peer in peers(axis):
            pl.semaphore_signal(barrier, inc=1, device_id={axis: peer}, device_id_type=MESH)
            greeted += 1

    def columns(index):
        return pl.ds(pl.multiple_of(index * fw, LANES), fw)

    tok_copy = pltpu.make_async_copy(tokens.at[:, columns(section)], tokv, loc_sem.at[0])
    cot_copy = pltpu.make_async_copy(cotangent.at[:, columns(section)], cotv, loc_sem.at[1])
    tok_copy.start()
    cot_copy.start()

    early = lax.broadcasted_iota(jnp.int32, (count, count), 0)
    late = lax.broadcasted_iota(jnp.int32, (count, count), 1)
    shift = MTOK.bit_length() - 1
    before = (own_col[...] == own_row[...]) & (early < late) & ((early >> shift) == (late >> shift))
    rank_in = jnp.sum(jnp.where(before, 1.0, 0.0), 0, keepdims=True)
    micro_of = (lax.broadcasted_iota(jnp.int32, (1, count), 1) >> shift).astype(jnp.float32)
    place = micro_of * cap + rank_in
    spots = lax.broadcasted_iota(jnp.int32, (spad, count), 0).astype(jnp.float32)
    fits = place == spots
    member = jnp.concatenate(
        [jnp.where(fits & (own_row[...] == d), 1.0, 0.0) for d in range(groups)], 0
    )
    flag = jnp.sum(member * choose_row[...].astype(jnp.float32), 1, keepdims=True)
    member = member.astype(jnp.bfloat16)

    tok_copy.wait()
    cot_copy.wait()
    contract_mid = ((1,), (0,))
    sendbuf[:, :, 0:fw] = (
        matmul(member, tokv[...], contract_mid).astype(jnp.bfloat16).reshape(groups, spad, fw)
    )
    sendbuf[:, :, fw : 2 * fw] = (
        matmul(member, cotv[...], contract_mid).astype(jnp.bfloat16).reshape(groups, spad, fw)
    )
    sendbuf[:, :, 2 * fw :] = (
        jnp.broadcast_to(flag, (groups * spad, LANES))
        .astype(jnp.bfloat16)
        .reshape(groups, spad, LANES)
    )

    pl.semaphore_wait(barrier, greeted)

    for _, peer in peers("dp"):
        pltpu.make_async_remote_copy(
            sendbuf.at[peer], recvbuf.at[dp], tok_s, tok_r, {"dp": peer}, MESH
        ).start()
    recvbuf[dp] = sendbuf[dp]

    down_scaled[...] = (down[...].astype(jnp.float32) * gains[...].astype(jnp.float32)).astype(
        jnp.bfloat16
    )
    for source, target, send, recv in (
        (down_scaled, w_down, wd_s, wd_r),
        (up, w_up, wu_s, wu_r),
    ):
        for _, peer in peers("section"):
            pltpu.make_async_remote_copy(
                source.at[:, columns(peer)],
                target.at[section],
                send,
                recv.at[section],
                {"section": peer},
                MESH,
            ).start()
        pltpu.make_async_copy(
            source.at[:, columns(section)], target.at[section], recv.at[section]
        ).start()

    drain(recvbuf.at[pl.ds(0, groups - 1)], tok_r)
    arrived = matmul(
        compact[...], recvbuf[...].reshape(groups * spad, 2 * fw + LANES), contract_mid
    )
    cur[...] = arrived[:, 0:fw]
    first_cot[...] = arrived[:, fw : 2 * fw]
    lane = lax.broadcasted_iota(jnp.int32, (slots, LANES), 1)
    second = arrived[:, 2 * fw :] > 0.5
    mask[...] = jnp.where(second == (lane >= LANES // 2), 1.0, 0.0)

    low = lax.broadcasted_iota(jnp.int32, (half, LANES), 1) < LANES // 2
    tall = lax.broadcasted_iota(jnp.int32, (TILE, LANES), 1)

    def packed(total):
        kept = total * mask[...]
        both = kept + pltpu.roll(kept, LANES // 2, 1)
        return jnp.where(low, both[0:half], both[half:])

    def unpacked(total):
        turned = pltpu.roll(total, LANES // 2, 1)
        both = jnp.concatenate(
            [jnp.where(low, total, turned), jnp.where(low, turned, total)], 0
        )
        return both * mask[...]

    def start_stage(axis, layer, slot, mine, theirs, send, recv):
        for place_at, peer in peers(axis):
            pltpu.make_async_remote_copy(
                mine.at[layer],
                theirs.at[layer, place_at],
                send,
                recv.at[slot],
                {axis: peer},
                MESH,
            ).start()

    def end_stage(layer, slot, theirs, recv):
        drain(theirs.at[layer], recv.at[slot])
        return sum(theirs[layer, i].astype(jnp.float32) for i in range(theirs.shape[1]))

    def forward(layer, _):
        x = cur[...]
        x_low = x.astype(jnp.bfloat16)
        xs[layer] = x_low
        squares = jnp.sum(x * x, 1, keepdims=True)
        folded = jnp.zeros((TILE, LANES), jnp.float32)
        for q in range(slots // TILE):
            folded = jnp.where(tall == q, squares[q * TILE : (q + 1) * TILE], folded)
        drain(w_down.at[layer], wd_r.at[layer])
        part = packed(matmul(x_low, w_down[layer], ((1,), (1,))))
        part = jnp.concatenate([part, folded], 0)
        p1[layer] = part.astype(jnp.bfloat16)
        start_stage("tensor", layer, layer, p1, f1, ss1, rs1)
        part = part + end_stage(layer, layer, f1, rs1)
        p2[layer] = part.astype(jnp.bfloat16)
        start_stage("section", layer, layer, p2, f2, ss2, rs2)
        part = part + end_stage(layer, layer, f2, rs2)
        folded = part[half:]
        squares = jnp.concatenate(
            [
                jnp.sum(jnp.where(tall == q, folded, 0.0), 1, keepdims=True)
                for q in range(slots // TILE)
            ],
            0,
        )
        scale_rows = lax.rsqrt(squares / width + EPS)
        rs[layer] = jnp.broadcast_to(scale_rows, (slots, LANES))
        latent = (unpacked(part[0:half]) * scale_rows).astype(jnp.bfloat16)
        zs[layer] = latent
        drain(w_up.at[layer], wu_r.at[layer])

        @pl.when(layer < layers - 1)
        def _():
            cur[...] = x + SCALE * matmul(latent, w_up[layer], contract_mid)

        return 0

    lax.fori_loop(0, layers, forward, 0)

    cur[...] = first_cot[...]

    def give_back(layer, product, store, target, send, recv):
        store[layer] = product.astype(jnp.bfloat16)

        @pl.when(layer == section)
        def _():
            pltpu.make_async_copy(store.at[layer], target.at[:, columns(section)], recv).start()

        @pl.when(layer != section)
        def _():
            pltpu.make_async_remote_copy(
                store.at[layer],
                target.at[:, columns(section)],
                send,
                recv,
                {"section": layer},
                MESH,
            ).start()

    contract_rows = ((0,), (0,))

    def backward(step, rank_gradient):
        layer = layers - 1 - step
        g = cur[...]
        g_low = g.astype(jnp.bfloat16)
        part = packed(matmul(g_low, w_up[layer], ((1,), (1,))))
        q1[layer] = part.astype(jnp.bfloat16)
        start_stage("tensor", layer, layers + layer, q1, h1, ss1, rs1)
        latent = zs[layer]
        give_back(
            layer,
            SCALE * matmul(latent, g_low, contract_rows),
            back_u,
            grad_up,
            gu_s,
            gu_r,
        )
        part = part + end_stage(layer, layers + layer, h1, rs1)
        q2[layer] = part.astype(jnp.bfloat16)
        start_stage("section", layer, layers + layer, q2, h2, ss2, rs2)

        @pl.when(step > 0)
        def _():
            give_back(
                layer + 1,
                matmul(rank_gradient, xs[layer + 1], contract_rows),
                back_d,
                grad_down,
                gd_s,
                gd_r,
            )

        part = part + end_stage(layer, layers + layer, h2, rs2)
        rank_low = (SCALE * unpacked(part)).astype(jnp.bfloat16)
        scale_rows = rs[layer][:, 0:1]
        product = rank_low.astype(jnp.float32) * latent.astype(jnp.float32)
        slope_rows[layer, :, 0:slots] = lax.dot_general(
            jnp.full((8, LANES), 1.0 / math.sqrt(width), jnp.float32),
            product,
            (((1,), (1,)), ((), ())),
            preferred_element_type=jnp.float32,
            precision=lax.Precision.HIGHEST,
        )

        @pl.when(layer > 0)
        def _():
            inner = jnp.sum(product, 1, keepdims=True) / width
            cur[...] = (
                g
                + scale_rows * matmul(rank_low, w_down[layer], contract_mid)
                - (scale_rows * scale_rows * inner) * xs[layer].astype(jnp.float32)
            )

        return (rank_low.astype(jnp.float32) * scale_rows).astype(jnp.bfloat16)

    rank_gradient = lax.fori_loop(
        0, layers, backward, jnp.zeros((slots, LANES), jnp.bfloat16)
    )
    give_back(0, matmul(rank_gradient, xs[0], contract_rows), back_d, grad_down, gd_s, gd_r)

    for _, peer in peers("dp"):
        pltpu.make_async_remote_copy(
            slope_rows.at[section], slopes.at[dp], sl_s, sl_r, {"dp": peer}, MESH
        ).start()
    slopes[dp] = slope_rows[section]

    drain(recvbuf.at[pl.ds(0, groups - 1)], tok_s)
    drain(w_down.at[pl.ds(0, layers - 1)], wd_s)
    drain(w_up.at[pl.ds(0, layers - 1)], wu_s)
    drain(f1, ss1)
    drain(h1, ss1)
    drain(f2, ss2)
    drain(h2, ss2)
    drain(back_d.at[pl.ds(0, layers - 1)], gd_s)
    drain(back_u.at[pl.ds(0, layers - 1)], gu_s)
    drain(slopes.at[pl.ds(0, groups - 1)], sl_s)
    drain(grad_up, gu_r)
    drain(grad_down, gd_r)
    drain(slopes.at[pl.ds(0, groups - 1)], sl_r)


def on_device(
    tokens,
    owner_indices,
    local_adapter_index,
    gains,
    adapter_down_weights,
    adapter_up_weights,
    cotangent,
):
    groups, layers, ranks = (lax.axis_size(a) for a in ("dp", "section", "tensor"))
    count, local = tokens.shape
    micro = count // MTOK
    cap = 5 * MTOK // (4 * groups)
    each = micro * cap
    spad = round_up(each, TILE)
    slots = groups * each
    fw = local // layers
    adapters, rank = adapter_down_weights.shape[1:3]
    rows = adapters * rank
    half = slots // 2
    down = adapter_down_weights.reshape(rows, local)
    up = adapter_up_weights.reshape(rows, local)
    own_row = owner_indices.reshape(1, count)
    choose_row = local_adapter_index.reshape(1, count)
    slot_ids = np.arange(slots)
    compact = np.zeros((slots, groups * spad), np.float32)
    compact[slot_ids, slot_ids // each * spad + slot_ids % each] = 1.0
    wide = round_up(slots, LANES)
    vmem = pl.BlockSpec(memory_space=pltpu.VMEM)
    anywhere = pl.BlockSpec(memory_space=pl.ANY)
    b16, f32 = jnp.bfloat16, jnp.float32
    dma = pltpu.SemaphoreType.DMA
    high = half + TILE
    grad_down, grad_up, slopes = pl.pallas_call(
        functools.partial(kernel, cap),
        out_shape=(
            jax.ShapeDtypeStruct((rows, local), b16),
            jax.ShapeDtypeStruct((rows, local), b16),
            jax.ShapeDtypeStruct((groups, 8, wide), f32),
        ),
        in_specs=[vmem] * 6 + [anywhere] * 3,
        out_specs=(vmem, vmem, vmem),
        scratch_shapes=[
            pltpu.VMEM((groups, spad, 2 * fw + LANES), b16),
            pltpu.VMEM((groups, spad, 2 * fw + LANES), b16),
            pltpu.VMEM((count, fw), b16),
            pltpu.VMEM((count, fw), b16),
            pltpu.VMEM((rows, local), b16),
            pltpu.VMEM((layers, rows, fw), b16),
            pltpu.VMEM((layers, rows, fw), b16),
            pltpu.VMEM((layers, high, LANES), b16),
            pltpu.VMEM((layers, ranks - 1, high, LANES), b16),
            pltpu.VMEM((layers, high, LANES), b16),
            pltpu.VMEM((layers, layers - 1, high, LANES), b16),
            pltpu.VMEM((layers, half, LANES), b16),
            pltpu.VMEM((layers, ranks - 1, half, LANES), b16),
            pltpu.VMEM((layers, half, LANES), b16),
            pltpu.VMEM((layers, layers - 1, half, LANES), b16),
            pltpu.VMEM((layers, slots, fw), b16),
            pltpu.VMEM((layers, slots, LANES), b16),
            pltpu.VMEM((layers, slots, LANES), f32),
            pltpu.VMEM((slots, fw), f32),
            pltpu.VMEM((slots, fw), f32),
            pltpu.VMEM((slots, LANES), f32),
            pltpu.VMEM((layers, rows, fw), b16),
            pltpu.VMEM((layers, rows, fw), b16),
            pltpu.VMEM((layers, 8, wide), f32),
            dma((2,)),
            dma,
            dma,
            dma,
            dma,
            dma((layers,)),
            dma((layers,)),
            dma,
            dma((2 * layers,)),
            dma,
            dma((2 * layers,)),
            dma,
            dma,
            dma,
            dma,
            dma,
            dma,
        ],
        compiler_params=pltpu.CompilerParams(
            collective_id=0, has_side_effects=True, vmem_limit_bytes=40 * 1024 * 1024
        ),
    )(
        owner_indices,
        own_row,
        choose_row,
        gains,
        down,
        jnp.asarray(compact, b16),
        tokens,
        cotangent,
        up,
    )
    grad_down = (grad_down.astype(f32) * gains.astype(f32)).astype(b16)
    own = owner_indices[:, 0]
    own_micro = own.reshape(micro, MTOK)
    same = own_micro[:, :, None] == own_micro[:, None, :]
    earlier = jnp.arange(MTOK)[:, None] > jnp.arange(MTOK)[None, :]
    rank_in = jnp.sum((same & earlier).astype(jnp.int32), 2).reshape(count)
    spot = lax.axis_index("dp") * each + jnp.arange(count) // MTOK * cap + rank_in
    here = (jnp.arange(groups)[None, :, None] == own[:, None, None]) & (
        jnp.arange(wide)[None, None, :] == spot[:, None, None]
    )
    slope = jnp.sum(jnp.where(here, slopes[None, :, 0, :], 0.0), (1, 2))
    shape = (1, adapters, rank, local)
    return (grad_down.reshape(shape), grad_up.reshape(shape), slope[None])


def solution(mesh):
    return jax.shard_map(
        on_device,
        mesh=mesh,
        in_specs=(
            P("dp", "tensor"),
            P("dp", None),
            P("dp"),
            P("section", "tensor"),
            P("section", "dp", None, "tensor"),
            P("section", "dp", None, "tensor"),
            P("dp", "tensor"),
        ),
        out_specs=(
            P("section", "dp", None, "tensor"),
            P("section", "dp", None, "tensor"),
            P("section", "dp"),
        ),
        check_vma=False,
    )
```

time: 1590 us -> 250 us (0.16)
  waiting for transfers between devices: 633 us -> 0 us
  blocking collectives: 427 us -> 0 us
  starting transfers between devices: 274 us -> 0 us
  Pallas kernels: 0 us -> 233 us
  local copies, waits for them, and re-layouts: 103 us -> 9.31 us
  matrix products: 65.6 us -> 0 us
  other arithmetic: 57.7 us -> 4.6 us
    all_to_all x45 -> x0, waiting for transfers between devices: 546 us -> none  [the longest x9 144 us: backward_step(): lax.all_to_all(outgoing.reshape(groups, cap, shard_width), 'dp', split_ax...]
    psum x36 -> x0, blocking collectives: 427 us -> none  [the longest x9 125 us: backward_step(): rank_gradient = lax.psum(partial_total_sum, 'tensor').astype(jnp.bfloat16)]
    pallas_call x0 -> x1, Pallas kernels: none -> 233 us  [on_device(): pl.pallas_call(functools.partial(kernel, cap), out_shape=(jax.ShapeDtypeS...]
    all_to_all x45 -> x0, starting transfers between devices: 222 us -> none  [the longest x9 84 us: forward_step(): lax.all_to_all(outgoing.reshape(groups, cap, shard_width), 'dp', split_ax...]
    ppermute x18 -> x0, waiting for transfers between devices: 87 us -> none  [shifted(): return lax.ppermute(x, axis, pairs)]
    dot_general x90 -> x0, matrix products: 65.6 us -> none  [the longest x18 16 us: expand_from_rank(): jnp.einsum('sr,ard->asd', rank_latent, weight, preferred_element_type=jnp...]
    ppermute x18 -> x0, starting transfers between devices: 52.4 us -> none  [shifted(): return lax.ppermute(x, axis, pairs)]
    dynamic_slice x46 -> x0, local copies, waits for them, and re-layouts: 30.2 us -> none  [the longest x18 13.2 us: routing(): own = lax.dynamic_slice_in_dim(owners, start, MTOK)]
  transfers between devices with their start and end apart: 63 -> 0, of which waited for: 54 -> 0; matrix products, arithmetic and copies ran while one was open for 5% -> 0% of each run, Pallas kernels for 0% -> 0%
where the time goes in v1:
time: 250 us; the launch traced here: 248 us
  Pallas kernels  233 us (93%)
  local copies, waits for them, and re-layouts  9.31 us (4%)
  other arithmetic  4.6 us (2%)
    pallas_call x1, Pallas kernels, on_device(): pl.pallas_call(functools.partial(kernel, cap), out_shape=(jax.ShapeDtypeS...  233 us
    unnamed x22, local copies, waits for them, and re-layouts  9.13 us

profile of v1, /device:TPU:1, one launch (start us, length us, event | category | flops | bytes accessed | tf_op | source)
XLA Modules:
  0.0 248.1 jit_solution(11892439305102517236)
XLA Ops:
  0.6 0.8 copy.12.own_col
  1.4 0.0 copy-start
  1.4 1.0 copy-done
  2.4 0.0 copy-start.1
  2.4 1.0 copy-done.1
  3.5 1.0 copy-done.2
  4.5 1.0 copy-done.3
  5.6 0.9 copy-done.4
  6.5 0.7 copy-done.5
  7.1 0.7 copy-done.6
  7.8 0.7 copy-done.8
  8.5 233.5 %shard_map.106 = (bf16[128,2048]{1,0:T(8,128)(2,1)S(1)}, bf16[128,2048]{1,0:T(8,128)(2,1)S(1)}, f32[16,8,256]{2,1,0:T(8,128)S(1)}) custom-call(s32[128,1]{1,0:T(8,128)S(1)} %copy.12.own_col, s32[1,128]{1,0:T(1,128)S(1)} %bitcast.16, s32[1,128]{1,0:T(1,128)S(1)} %bitcast.18, bf16[1,2048]{1,0:T(2,128)(2,1)S(1)} %copy-done.5, bf16[128,2048]{1,0:T(8,128)(2,1)S(1)} %bitcast.14, ...), custom_call_target="tpu_custom_call" | custom-call | tf_op jit(solution)/shard_map/pallas_call | solution.py:391
  241.9 0.0 copy-start.7
  241.9 0.9 multiply_convert_fusion
  242.9 0.5 broadcast.76
  243.4 0.0 copy-done.7
  243.4 0.7 reduce.3
  244.1 0.1 eq.55
  244.1 0.2 convert_reduce_fusion
  244.3 0.1 reshape.117
  244.4 0.1 iota_compare_fusion
  244.5 0.1 iota_compare_fusion.1
  244.6 2.7 %select_reduce_fusion = f32[128]{0:T(128)} fusion(f32[16,256]{1,0:T(8,128)S(1)} %bitcast.20, pred[128,256]{1,0:T(8,128)(4,1)S(1)} %iota_compare_fusion, pred[128,16]{1,0:T(8,128)(4,1)S(1)} %iota_compare_fusion.1), kind=kLoop, calls=%fused_computation | loop fusion | flops 1572736 | bytes 51712 | tf_op jit(solution)/shard_map/reduce_sum | solution.py:467
  247.3 0.8 copy.17
  (11 shorter events, 0.1 us)
Async XLA Ops:
  1.4 1.0 copy-start
  2.4 1.0 copy-start.1
  3.5 1.0 copy-start.2
  4.5 1.0 copy-start.3
  5.6 0.9 copy-start.4
  6.4 0.7 copy-start.5
  7.1 0.7 copy-start.6
  7.8 0.7 copy-start.8
  241.9 1.5 copy-start.7

commit v2 on v1

v2 whole, which is shorter than its diff:
```python
import functools
import math

import jax
import jax.numpy as jnp
import numpy as np
from jax import lax
from jax.experimental import pallas as pl
from jax.experimental.pallas import tpu as pltpu
from jax.sharding import PartitionSpec as P

MTOK = 64
LANES = 128
TILE = 16
EPS = 1e-05
SCALE = 0.5
MESH = pl.DeviceIdType.MESH
NN = ((1,), (0,))
NT = ((1,), (1,))
TN = ((0,), (0,))


def round_up(value, unit):
    return -(-value // unit) * unit


def matmul(a, b, contract):
    return lax.dot_general(a, b, (contract, ((), ())), preferred_element_type=jnp.float32)


def drain(ref, sem):
    pltpu.make_async_copy(ref, ref, sem).wait()


def peers(axis):
    count, me = lax.axis_size(axis), lax.axis_index(axis)
    return [lax.rem(me + o, count) for o in range(1, count)]


def payload_rows(layers, half, rank):
    at, rows = {}, 0
    at["squares"], rows = rows, rows + TILE
    for name, count in (("p", layers), ("q", layers - 1), ("r", layers)):
        at[name], rows = rows, rows + count * half
    for k in range(layers - 1):
        for name, others in (("m", range(k + 1, layers)), ("u", range(k, layers - 1))):
            for other in others:
                at[name, k, other], rows = rows, rows + rank
    return at, rows


def kernel(
    cap,
    own,
    choose,
    gains,
    down,
    compact,
    tokens,
    cotangent,
    up,
    grad_down,
    grad_up,
    slope_out,
    own_v,
    choose_v,
    gains_v,
    down_v,
    compact_v,
    tokv,
    cotv,
    sendbuf,
    recvbuf,
    down_scaled,
    w_down,
    w_up,
    part,
    fin,
    got,
    got_y,
    acc_p,
    acc_q,
    acc_w,
    seen,
    big_m,
    big_u,
    xs,
    zs,
    rd,
    es,
    prods,
    first_x,
    first_cot,
    mask,
    back_d,
    back_u,
    slope_row,
    slopes,
    loc_sem,
    tok_s,
    tok_r,
    wd_s,
    wu_s,
    wd_r,
    wu_r,
    ar_s,
    ar_r,
    gd_s,
    gu_s,
    gd_r,
    gu_r,
    sl_s,
    sl_r,
):
    dp = lax.axis_index("dp")
    section = lax.axis_index("section")
    tensor = lax.axis_index("tensor")
    groups = lax.axis_size("dp")
    layers = lax.axis_size("section")
    ranks = lax.axis_size("tensor")
    bits = ranks.bit_length() - 1
    count = tokens.shape[0]
    fw = tokv.shape[1]
    width = tokens.shape[1] * ranks
    spad = sendbuf.shape[1]
    slots = xs.shape[1]
    half = slots // 2
    rank = LANES // 2
    each = slots // groups
    bf16, f32 = jnp.bfloat16, jnp.float32
    at, _ = payload_rows(layers, half, rank)

    barrier = pltpu.get_barrier_semaphore()
    greeted = 0
    for axis in ("tensor", "section", "dp"):
        for peer in peers(axis):
            pl.semaphore_signal(barrier, inc=1, device_id={axis: peer}, device_id_type=MESH)
            greeted += 1

    def columns(index):
        return pl.ds(pl.multiple_of(index * fw, LANES), fw)

    loads = [
        pltpu.make_async_copy(source, target, loc_sem.at[i])
        for i, (source, target) in enumerate(
            (
                (own, own_v),
                (choose, choose_v),
                (tokens.at[:, columns(section)], tokv),
                (cotangent.at[:, columns(section)], cotv),
                (gains, gains_v),
                (down, down_v),
                (compact, compact_v),
            )
        )
    ]
    for load in loads:
        load.start()

    early = lax.broadcasted_iota(jnp.int32, (count, count), 0)
    late = lax.broadcasted_iota(jnp.int32, (count, count), 1)
    diagonal = early == late
    shift = MTOK.bit_length() - 1
    loads[0].wait()
    loads[1].wait()
    own_row = own_v[...].astype(f32)
    own_col = jnp.sum(jnp.where(diagonal, own_row, 0.0), 1, keepdims=True)
    before = (own_col == own_row) & (early < late) & ((early >> shift) == (late >> shift))
    rank_in = jnp.sum(jnp.where(before, 1.0, 0.0), 0, keepdims=True)
    micro_of = (lax.broadcasted_iota(jnp.int32, (1, count), 1) >> shift).astype(f32)
    place = micro_of * cap + rank_in
    spots = lax.broadcasted_iota(jnp.int32, (spad, count), 0).astype(f32)
    fits = place == spots
    member = jnp.concatenate(
        [jnp.where(fits & (own_row == d), 1.0, 0.0) for d in range(groups)], 0
    )
    flag = jnp.sum(member * choose_v[...].astype(f32), 1, keepdims=True)
    member = member.astype(bf16)
    loads[2].wait()
    loads[3].wait()
    sendbuf[:, :, 0:fw] = matmul(member, tokv[...], NN).astype(bf16).reshape(groups, spad, fw)
    sendbuf[:, :, fw : 2 * fw] = (
        matmul(member, cotv[...], NN).astype(bf16).reshape(groups, spad, fw)
    )
    sendbuf[:, :, 2 * fw :] = (
        jnp.broadcast_to(flag, (groups * spad, LANES)).astype(bf16).reshape(groups, spad, LANES)
    )

    pl.semaphore_wait(barrier, greeted)

    for peer in peers("dp"):
        pltpu.make_async_remote_copy(
            sendbuf.at[peer], recvbuf.at[dp], tok_s, tok_r, {"dp": peer}, MESH
        ).start()
    recvbuf[dp] = sendbuf[dp]

    def spread(source, target, send, recv):
        for peer in peers("section"):
            pltpu.make_async_remote_copy(
                source.at[:, columns(peer)],
                target.at[section],
                send,
                recv.at[section],
                {"section": peer},
                MESH,
            ).start()
        pltpu.make_async_copy(
            source.at[:, columns(section)], target.at[section], recv.at[section]
        ).start()

    spread(up, w_up, wu_s, wu_r)
    for load in loads[4:]:
        load.wait()
    down_scaled[...] = (down_v[...].astype(f32) * gains_v[...].astype(f32)).astype(bf16)
    spread(down_scaled, w_down, wd_s, wd_r)

    drain(recvbuf.at[pl.ds(0, groups - 1)], tok_r)
    arrived = matmul(compact_v[...], recvbuf[...].reshape(groups * spad, 2 * fw + LANES), NN)
    x0 = arrived[:, 0:fw]
    first_x[...] = x0
    first_cot[...] = arrived[:, fw : 2 * fw]
    lane = lax.broadcasted_iota(jnp.int32, (slots, LANES), 1)
    second = arrived[:, 2 * fw :] > 0.5
    mask[...] = jnp.where(second == (lane >= rank), 1.0, 0.0)

    low = lax.broadcasted_iota(jnp.int32, (half, LANES), 1) < rank
    low_rank = lax.broadcasted_iota(jnp.int32, (rank, LANES), 1) < rank
    tall = lax.broadcasted_iota(jnp.int32, (TILE, LANES), 1)

    def packed(total):
        kept = total * mask[...]
        both = kept + pltpu.roll(kept, rank, 1)
        return jnp.where(low, both[0:half], both[half:])

    def unpacked(total):
        turned = pltpu.roll(total, rank, 1)
        both = jnp.concatenate([jnp.where(low, total, turned), jnp.where(low, turned, total)], 0)
        return both * mask[...]

    squares = jnp.sum(x0 * x0, 1, keepdims=True)
    folded = jnp.zeros((TILE, LANES), f32)
    for q in range(slots // TILE):
        folded = jnp.where(tall == q, squares[q * TILE : (q + 1) * TILE], folded)
    part[0:TILE] = folded.astype(bf16)

    for layer in range(layers):
        drain(w_up.at[layer], wu_r.at[layer])
    x_low = first_x[...].astype(bf16)
    cot_low = first_cot[...].astype(bf16)
    for layer in range(layers):
        weight = w_up[layer]
        if layer < layers - 1:
            row = at["q"] + layer * half
            part[row : row + half] = packed(matmul(x_low, weight, NT)).astype(bf16)
        row = at["r"] + layer * half
        part[row : row + half] = packed(matmul(cot_low, weight, NT)).astype(bf16)

    def pairs(name, k, others, weights):
        first, last = others[0], others[-1] + 1
        stacked = weights[first:last].reshape((last - first) * LANES, fw)
        product = matmul(w_up[k], stacked, NT)
        for i, other in enumerate(others):
            block = product[:, i * LANES : (i + 1) * LANES]
            row = at[name, k, other]
            part[row : row + rank] = jnp.where(low_rank, block[0:rank], block[rank:]).astype(bf16)

    for k in range(layers - 1):
        pairs("u", k, range(k, layers - 1), w_up)
    for layer in range(layers):
        drain(w_down.at[layer], wd_r.at[layer])
    for layer in range(layers):
        row = at["p"] + layer * half
        part[row : row + half] = packed(matmul(x_low, w_down[layer], NT)).astype(bf16)
    for k in range(layers - 1):
        pairs("m", k, range(k + 1, layers), w_down)

    total_rows = part.shape[0]
    piece = total_rows // (ranks * layers)

    def rows(first, size):
        return pl.ds(pl.multiple_of(first, TILE), size)

    base, size, stage, starts = 0, total_rows, 0, []
    for bit in range(bits):
        size //= 2
        mine = (tensor >> bit) & 1
        keep, give = base + mine * size, base + (1 - mine) * size
        peer = tensor ^ (1 << bit)
        spot = total_rows - 2 * size
        pltpu.make_async_remote_copy(
            part.at[rows(give, size)],
            got.at[pl.ds(spot, size)],
            ar_s.at[stage],
            ar_r.at[stage],
            {"tensor": peer},
            MESH,
        ).start()
        drain(got.at[pl.ds(spot, size)], ar_r.at[stage])
        part[rows(keep, size)] = (
            part[rows(keep, size)].astype(f32) + got[spot : spot + size].astype(f32)
        ).astype(bf16)
        starts.append((keep, size, peer))
        base, stage = keep, stage + 1
    for o, peer in enumerate(peers("section")):
        pltpu.make_async_remote_copy(
            part.at[rows(base + peer * piece, piece)],
            got_y.at[o],
            ar_s.at[stage],
            ar_r.at[stage],
            {"section": peer},
            MESH,
        ).start()
    drain(got_y, ar_r.at[stage])
    mine = base + section * piece
    total = part[rows(mine, piece)].astype(f32)
    for o in range(layers - 1):
        total += got_y[o].astype(f32)
    fin[rows(mine, piece)] = total.astype(bf16)
    stage += 1
    for peer in peers("section"):
        pltpu.make_async_remote_copy(
            fin.at[rows(mine, piece)],
            fin.at[rows(mine, piece)],
            ar_s.at[stage],
            ar_r.at[stage],
            {"section": peer},
            MESH,
        ).start()
    drain(fin.at[pl.ds(0, (layers - 1) * piece)], ar_r.at[stage])
    stage += 1
    for keep, size, peer in reversed(starts):
        pltpu.make_async_remote_copy(
            fin.at[rows(keep, size)],
            fin.at[rows(keep, size)],
            ar_s.at[stage],
            ar_r.at[stage],
            {"tensor": peer},
            MESH,
        ).start()
        drain(fin.at[pl.ds(0, size)], ar_r.at[stage])
        stage += 1

    def lanes(first, last=None):
        return slice(first * LANES, (first + 1 if last is None else last) * LANES)

    for name, target, number in (
        ("p", acc_p, layers),
        ("q", acc_q, layers - 1),
        ("r", acc_w, layers),
    ):
        for layer in range(number):
            row = at[name] + layer * half
            target[:, lanes(layer)] = unpacked(fin[row : row + half].astype(f32))
    for k in range(layers - 1):
        for name, target, others in (
            ("m", big_m, range(k + 1, layers)),
            ("u", big_u, range(k, layers - 1)),
        ):
            for other in others:
                row = at[name, k, other]
                block = fin[row : row + rank]
                zero = jnp.zeros_like(block)
                target[k, 0:rank, lanes(other)] = jnp.where(low_rank, block, zero)
                target[k, rank:, lanes(other)] = jnp.where(low_rank, zero, block)
    folded = fin[0:TILE].astype(f32)
    squares = jnp.concatenate(
        [
            jnp.sum(jnp.where(tall == q, folded, 0.0), 1, keepdims=True)
            for q in range(slots // TILE)
        ],
        0,
    )

    scales = []
    for k in range(layers):
        scale_rows = lax.rsqrt(squares / width + EPS)
        scales.append(scale_rows)
        latent = (acc_p[:, lanes(k)] * scale_rows).astype(bf16)
        zs[k] = latent
        if k == layers - 1:
            break
        if k < layers - 1:
            acc_p[:, lanes(k + 1, layers)] += SCALE * matmul(
                latent, big_m[k, :, lanes(k + 1, layers)], NN
            )
            inner = acc_q[:, lanes(k)]
            step = SCALE * matmul(latent, big_u[k, :, lanes(k, layers - 1)], NN)
            squares = jnp.maximum(
                squares
                + jnp.sum(
                    latent.astype(f32) * (inner + 0.5 * step[:, 0:LANES]), 1, keepdims=True
                ),
                0.0,
            )
            acc_q[:, lanes(k, layers - 1)] += step
            if k > 0:
                others = big_u[0:k, :, lanes(k)].reshape(k * LANES, LANES)
                acc_q[:, lanes(0, k)] += SCALE * matmul(latent, others, NT)
            seen[k + 1, :, lanes(0, k + 1)] = acc_q[:, lanes(0, k + 1)].astype(bf16)

    for m in reversed(range(layers)):
        rank_low = (SCALE * acc_w[:, lanes(m)]).astype(bf16)
        product = rank_low.astype(f32) * zs[m].astype(f32)
        prods[m] = product
        scale_rows = scales[m]
        scaled = (rank_low.astype(f32) * scale_rows).astype(bf16)
        rd[m] = scaled
        if m > 0:
            weight = scale_rows * scale_rows * jnp.sum(product, 1, keepdims=True) / width
            es[m] = jnp.broadcast_to(weight, (slots, LANES))
            others = big_m[0:m, :, lanes(m)].reshape(m * LANES, LANES)
            acc_w[:, lanes(0, m)] += matmul(scaled, others, NT) - weight * seen[
                m, :, lanes(0, m)
            ].astype(f32)

    slope_row[:, 0:slots] = lax.dot_general(
        jnp.full((8, LANES), 1.0 / math.sqrt(width), f32),
        prods[section],
        (NT, ((), ())),
        preferred_element_type=f32,
        precision=lax.Precision.HIGHEST,
    )
    for peer in peers("dp"):
        pltpu.make_async_remote_copy(
            slope_row, slopes.at[dp], sl_s, sl_r, {"dp": peer}, MESH
        ).start()
    slopes[dp] = slope_row[...]

    x = first_x[...]
    for layer in range(layers):
        xs[layer] = x.astype(bf16)
        if layer < layers - 1:
            x = x + SCALE * matmul(zs[layer], w_up[layer], NN)

    def give_back(layer, product, store, target, send, recv):
        store[layer] = product.astype(bf16)

        @pl.when(section == layer)
        def _():
            pltpu.make_async_copy(store.at[layer], target.at[:, columns(section)], recv).start()

        @pl.when(section != layer)
        def _():
            pltpu.make_async_remote_copy(
                store.at[layer],
                target.at[:, columns(section)],
                send,
                recv,
                {"section": layer},
                MESH,
            ).start()

    g = first_cot[...]
    for layer in reversed(range(layers)):
        g_low = g.astype(bf16)
        give_back(layer, SCALE * matmul(zs[layer], g_low, TN), back_u, grad_up, gu_s, gu_r)
        give_back(layer, matmul(rd[layer], xs[layer], TN), back_d, grad_down, gd_s, gd_r)
        if layer > 0:
            g = (
                g
                + matmul(rd[layer], w_down[layer], NN)
                - es[layer][:, 0:1] * xs[layer].astype(f32)
            )

    drain(recvbuf.at[pl.ds(0, groups - 1)], tok_s)
    drain(w_down.at[pl.ds(0, layers - 1)], wd_s)
    drain(w_up.at[pl.ds(0, layers - 1)], wu_s)
    stage = 0
    for _, size, _ in starts:
        drain(got.at[pl.ds(0, size)], ar_s.at[stage])
        stage += 1
    for _ in range(2):
        drain(got_y, ar_s.at[stage])
        stage += 1
    for _, size, _ in reversed(starts):
        drain(got.at[pl.ds(0, size)], ar_s.at[stage])
        stage += 1
    drain(back_d.at[pl.ds(0, layers - 1)], gd_s)
    drain(back_u.at[pl.ds(0, layers - 1)], gu_s)
    drain(slopes.at[pl.ds(0, groups - 1)], sl_s)

    drain(slopes.at[pl.ds(0, groups - 1)], sl_r)
    wide = slopes.shape[2]
    found = jnp.zeros((count, wide), f32)
    for d in range(groups):
        found = jnp.where(own_col == d, slopes[d, 0:1], found)
    first_slot = (dp * each).astype(f32)
    place_col = jnp.sum(jnp.where(diagonal, place, 0.0), 1, keepdims=True) + first_slot
    here = lax.broadcasted_iota(jnp.int32, (count, wide), 1).astype(f32) == place_col
    slope_col = jnp.sum(jnp.where(here, found, 0.0), 1, keepdims=True)
    slope_out[...] = jnp.sum(jnp.where(diagonal, slope_col, 0.0), 0, keepdims=True)

    drain(grad_up, gu_r)
    drain(grad_down, gd_r)


def on_device(
    tokens,
    owner_indices,
    local_adapter_index,
    gains,
    adapter_down_weights,
    adapter_up_weights,
    cotangent,
):
    groups, layers, ranks = (lax.axis_size(a) for a in ("dp", "section", "tensor"))
    count, local = tokens.shape
    micro = count // MTOK
    cap = 5 * MTOK // (4 * groups)
    each = micro * cap
    spad = round_up(each, TILE)
    slots = groups * each
    fw = local // layers
    adapters, rank = adapter_down_weights.shape[1:3]
    weight_rows = adapters * rank
    half = slots // 2
    slot_ids = np.arange(slots)
    compact = np.zeros((slots, groups * spad), np.float32)
    compact[slot_ids, slot_ids // each * spad + slot_ids % each] = 1.0
    wide = round_up(slots, LANES)
    _, rows = payload_rows(layers, half, rank)
    rows = round_up(rows, TILE * layers * ranks)
    piece = rows // (layers * ranks)
    stages = 2 * (ranks.bit_length() - 1) + 2
    vmem = pl.BlockSpec(memory_space=pltpu.VMEM)
    anywhere = pl.BlockSpec(memory_space=pl.ANY)
    b16, f32 = jnp.bfloat16, jnp.float32
    dma = pltpu.SemaphoreType.DMA
    grad_down, grad_up, slope = pl.pallas_call(
        functools.partial(kernel, cap),
        out_shape=(
            jax.ShapeDtypeStruct((weight_rows, local), b16),
            jax.ShapeDtypeStruct((weight_rows, local), b16),
            jax.ShapeDtypeStruct((1, count), f32),
        ),
        in_specs=[anywhere] * 8,
        out_specs=(vmem, vmem, vmem),
        scratch_shapes=[
            pltpu.VMEM((1, count), jnp.int32),
            pltpu.VMEM((1, count), jnp.int32),
            pltpu.VMEM((1, local), b16),
            pltpu.VMEM((weight_rows, local), b16),
            pltpu.VMEM(compact.shape, b16),
            pltpu.VMEM((count, fw), b16),
            pltpu.VMEM((count, fw), b16),
            pltpu.VMEM((groups, spad, 2 * fw + LANES), b16),
            pltpu.VMEM((groups, spad, 2 * fw + LANES), b16),
            pltpu.VMEM((weight_rows, local), b16),
            pltpu.VMEM((layers, weight_rows, fw), b16),
            pltpu.VMEM((layers, weight_rows, fw), b16),
            pltpu.VMEM((rows, LANES), b16),
            pltpu.VMEM((rows, LANES), b16),
            pltpu.VMEM((rows, LANES), b16),
            pltpu.VMEM((layers - 1, piece, LANES), b16),
            pltpu.VMEM((slots, layers * LANES), f32),
            pltpu.VMEM((slots, layers * LANES), f32),
            pltpu.VMEM((slots, layers * LANES), f32),
            pltpu.VMEM((layers, slots, layers * LANES), b16),
            pltpu.VMEM((layers, LANES, layers * LANES), b16),
            pltpu.VMEM((layers, LANES, layers * LANES), b16),
            pltpu.VMEM((layers, slots, fw), b16),
            pltpu.VMEM((layers, slots, LANES), b16),
            pltpu.VMEM((layers, slots, LANES), b16),
            pltpu.VMEM((layers, slots, LANES), f32),
            pltpu.VMEM((layers, slots, LANES), f32),
            pltpu.VMEM((slots, fw), f32),
            pltpu.VMEM((slots, fw), f32),
            pltpu.VMEM((slots, LANES), f32),
            pltpu.VMEM((layers, weight_rows, fw), b16),
            pltpu.VMEM((layers, weight_rows, fw), b16),
            pltpu.VMEM((8, wide), f32),
            pltpu.VMEM((groups, 8, wide), f32),
            dma((7,)),
            dma,
            dma,
            dma,
            dma,
            dma((layers,)),
            dma((layers,)),
            dma((stages,)),
            dma((stages,)),
            dma,
            dma,
            dma,
            dma,
            dma,
            dma,
        ],
        compiler_params=pltpu.CompilerParams(
            collective_id=0, has_side_effects=True, vmem_limit_bytes=48 * 1024 * 1024
        ),
    )(
        owner_indices.reshape(1, count),
        local_adapter_index.reshape(1, count),
        gains,
        adapter_down_weights.reshape(weight_rows, local),
        jnp.asarray(compact, b16),
        tokens,
        cotangent,
        adapter_up_weights.reshape(weight_rows, local),
    )
    grad_down = (grad_down.astype(f32) * gains.astype(f32)).astype(b16)
    shape = (1, adapters, rank, local)
    return (grad_down.reshape(shape), grad_up.reshape(shape), slope)


def solution(mesh):
    return jax.shard_map(
        on_device,
        mesh=mesh,
        in_specs=(
            P("dp", "tensor"),
            P("dp", None),
            P("dp"),
            P("section", "tensor"),
            P("section", "dp", None, "tensor"),
            P("section", "dp", None, "tensor"),
            P("dp", "tensor"),
        ),
        out_specs=(
            P("section", "dp", None, "tensor"),
            P("section", "dp", None, "tensor"),
            P("section", "dp"),
        ),
        check_vma=False,
    )
```

time: 250 us -> 125 us (0.50)
  Pallas kernels: 233 us -> 115 us
  other arithmetic: 4.6 us -> 1.67 us
    pallas_call x1, Pallas kernels: 233 us -> 115 us  [on_device(): pl.pallas_call(functools.partial(kernel, cap), out_shape=(jax.ShapeDtypeS...]
    reduce_sum x2 -> x0, other arithmetic: 2.84 us -> none  [the longest x1 2.66 us: on_device(): slope = jnp.sum(jnp.where(here, slopes[None, :, 0, :], 0.0), (1, 2))]
    unnamed x22 -> x18, local copies, waits for them, and re-layouts: 9.13 us -> 7.01 us
where the time goes in v2:
time: 125 us
  Pallas kernels  115 us (92%)
  local copies, waits for them, and re-layouts  7.01 us (6%)
  other arithmetic  1.67 us (1%)
    pallas_call x1, Pallas kernels, on_device(): pl.pallas_call(functools.partial(kernel, cap), out_shape=(jax.ShapeDtypeS...  115 us
    unnamed x18, local copies, waits for them, and re-layouts  7.01 us

profile of v2, /device:TPU:1, one launch (start us, length us, event | category | flops | bytes accessed | tf_op | source)
XLA Modules:
  0.0 124.5 jit_solution(12855073398257901574)
XLA Ops:
  0.6 0.0 copy-start.5
  0.6 0.8 mul.17
  1.4 0.0 copy-start.6
  1.4 0.0 copy-start.7
  1.4 0.0 copy-done.5
  1.4 0.6 copy-done.6
  2.1 0.0 copy-done.7
  2.1 0.0 copy-start
  2.1 1.0 copy-done
  3.1 0.0 copy-start.1
  3.1 1.0 copy-done.1
  4.2 0.0 copy-start.2
  4.2 1.0 copy-done.2
  5.2 0.0 copy-start.3
  5.2 1.0 copy-done.3
  6.3 0.0 copy-start.4
  6.3 0.9 copy-done.4
  7.1 115.2 %shard_map.103 = (bf16[128,2048]{1,0:T(8,128)(2,1)S(1)}, bf16[128,2048]{1,0:T(8,128)(2,1)S(1)}, f32[1,128]{1,0:T(1,128)S(1)}) custom-call(s32[1,128]{1,0:T(1,128)S(1)} %bitcast.10, s32[1,128]{1,0:T(1,128)S(1)} %bitcast.11, bf16[1,2048]{1,0:T(2,128)(2,1)S(1)} %copy-done.5, bf16[128,2048]{1,0:T(8,128)(2,1)S(1)} %bitcast.8, bf16[160,256]{1,0:T(8,128)(2,1)S(1)} %copy-done.4, ...), custom_call_target="tpu_custom_call" | custom-call | tf_op jit(solution)/shard_map/pallas_call | solution.py:529
  122.3 0.9 multiply_convert_fusion
  123.2 0.8 copy.13
  124.0 0.5 copy.14
Async XLA Ops:
  0.6 0.8 copy-start.5
  1.4 0.7 copy-start.6
  1.4 0.7 copy-start.7
  2.1 1.0 copy-start
  3.1 1.0 copy-start.1
  4.2 1.0 copy-start.2
  5.2 1.0 copy-start.3
  6.3 0.9 copy-start.4

commit v3 on v2

--- a/solution.py
+++ b/solution.py
@@ -37,16 +37,19 @@
     return [lax.rem(me + o, count) for o in range(1, count)]
 
 
-def payload_rows(layers, half, rank):
-    at, rows = {}, 0
-    at["squares"], rows = rows, rows + TILE
-    for name, count in (("p", layers), ("q", layers - 1), ("r", layers)):
+def payload_rows(layers, half, rank, unit):
+    at, ends = {}, []
+    at["squares"], rows = 0, TILE
+    for number, name, count in (("u", "q", layers - 1), ("m", "p", layers)):
         at[name], rows = rows, rows + count * half
-    for k in range(layers - 1):
-        for name, others in (("m", range(k + 1, layers)), ("u", range(k, layers - 1))):
-            for other in others:
-                at[name, k, other], rows = rows, rows + rank
-    return at, rows
+        if number == "u":
+            at["r"], rows = rows, rows + layers * half
+        for k in range(layers - 1):
+            for other in range(k, layers - 1) if number == "u" else range(k + 1, layers):
+                at[number, k, other], rows = rows, rows + rank
+        rows = round_up(rows, unit)
+        ends.append(rows)
+    return at, ends
 
 
 def kernel(
@@ -85,6 +88,7 @@
     big_m,
     big_u,
     xs,
+    gs,
     zs,
     rd,
     es,
@@ -128,7 +132,7 @@
     rank = LANES // 2
     each = slots // groups
     bf16, f32 = jnp.bfloat16, jnp.float32
-    at, _ = payload_rows(layers, half, rank)
+    at, ends = payload_rows(layers, half, rank, TILE * layers * ranks)
 
     barrier = pltpu.get_barrier_semaphore()
     greeted = 0
@@ -156,6 +160,28 @@
     ]
     for load in loads:
         load.start()
+
+    pl.semaphore_wait(barrier, greeted)
+
+    def spread(source, target, send, recv):
+        for peer in peers("section"):
+            pltpu.make_async_remote_copy(
+                source.at[:, columns(peer)],
+                target.at[section],
+                send,
+                recv.at[section],
+                {"section": peer},
+                MESH,
+            ).start()
+        pltpu.make_async_copy(
+            source.at[:, columns(section)], target.at[section], recv.at[section]
+        ).start()
+
+    spread(up, w_up, wu_s, wu_r)
+    for load in loads[4:]:
+        load.wait()
+    down_scaled[...] = (down_v[...].astype(f32) * gains_v[...].astype(f32)).astype(bf16)
+    spread(down_scaled, w_down, wd_s, wd_r)
 
     early = lax.broadcasted_iota(jnp.int32, (count, count), 0)
     late = lax.broadcasted_iota(jnp.int32, (count, count), 1)
@@ -186,33 +212,11 @@
         jnp.broadcast_to(flag, (groups * spad, LANES)).astype(bf16).reshape(groups, spad, LANES)
     )
 
-    pl.semaphore_wait(barrier, greeted)
-
     for peer in peers("dp"):
         pltpu.make_async_remote_copy(
             sendbuf.at[peer], recvbuf.at[dp], tok_s, tok_r, {"dp": peer}, MESH
         ).start()
     recvbuf[dp] = sendbuf[dp]
-
-    def spread(source, target, send, recv):
-        for peer in peers("section"):
-            pltpu.make_async_remote_copy(
-                source.at[:, columns(peer)],
-                target.at[section],
-                send,
-                recv.at[section],
-                {"section": peer},
-                MESH,
-            ).start()
-        pltpu.make_async_copy(
-            source.at[:, columns(section)], target.at[section], recv.at[section]
-        ).start()
-
-    spread(up, w_up, wu_s, wu_r)
-    for load in loads[4:]:
-        load.wait()
-    down_scaled[...] = (down_v[...].astype(f32) * gains_v[...].astype(f32)).astype(bf16)
-    spread(down_scaled, w_down, wd_s, wd_r)
 
     drain(recvbuf.at[pl.ds(0, groups - 1)], tok_r)
     arrived = matmul(compact_v[...], recvbuf[...].reshape(groups * spad, 2 * fw + LANES), NN)
@@ -266,6 +270,74 @@
 
     for k in range(layers - 1):
         pairs("u", k, range(k, layers - 1), w_up)
+
+    def rows(first, size):
+        return pl.ds(pl.multiple_of(first, TILE), size)
+
+    def all_reduce(chunk):
+        first = ends[chunk - 1] if chunk else 0
+        size = ends[chunk] - first
+        whole, piece, y_first = size, size // (ranks * layers), first // (ranks * layers)
+        base, stage, starts = first, 0, []
+        sends, arrivals = ar_s.at[chunk], ar_r.at[chunk]
+
+        def send(source, target, device):
+            pltpu.make_async_remote_copy(
+                source, target, sends.at[stage], arrivals.at[stage], device, MESH
+            ).start()
+
+        for bit in range(bits):
+            size //= 2
+            mine = (tensor >> bit) & 1
+            keep, give = base + mine * size, base + (1 - mine) * size
+            peer = tensor ^ (1 << bit)
+            spot = first + whole - 2 * size
+            send(part.at[rows(give, size)], got.at[pl.ds(spot, size)], {"tensor": peer})
+            yield
+            drain(got.at[pl.ds(spot, size)], arrivals.at[stage])
+            part[rows(keep, size)] = (
+                part[rows(keep, size)].astype(f32) + got[spot : spot + size].astype(f32)
+            ).astype(bf16)
+            starts.append((keep, size, peer))
+            base, stage = keep, stage + 1
+        for o, peer in enumerate(peers("section")):
+            send(
+                part.at[rows(base + peer * piece, piece)],
+                got_y.at[o, pl.ds(y_first, piece)],
+                {"section": peer},
+            )
+        yield
+        drain(fin.at[pl.ds(first, (layers - 1) * piece)], arrivals.at[stage])
+        stage += 1
+        mine = base + section * piece
+        total = part[rows(mine, piece)].astype(f32)
+        for o in range(layers - 1):
+            total += got_y[o, y_first : y_first + piece].astype(f32)
+        fin[rows(mine, piece)] = total.astype(bf16)
+        for peer in peers("section"):
+            send(fin.at[rows(mine, piece)], fin.at[rows(mine, piece)], {"section": peer})
+        yield
+        drain(fin.at[pl.ds(first, (layers - 1) * piece)], arrivals.at[stage])
+        stage += 1
+        for keep, size, peer in reversed(starts):
+            send(fin.at[rows(keep, size)], fin.at[rows(keep, size)], {"tensor": peer})
+            yield
+            drain(fin.at[pl.ds(first, size)], arrivals.at[stage])
+            stage += 1
+        sizes = [size for _, size, _ in starts]
+        y_size = (layers - 1) * piece
+        for i, size in enumerate([*sizes, y_size, y_size, *reversed(sizes)]):
+            sent.append((first, size, sends.at[i]))
+
+    sent = []
+    early_half, late_half = all_reduce(0), all_reduce(1)
+
+    def advance(*halves):
+        for chunk in halves:
+            next(chunk, None)
+
+    for _ in range(bits + 1):
+        advance(early_half)
     for layer in range(layers):
         drain(w_down.at[layer], wd_r.at[layer])
     for layer in range(layers):
@@ -273,72 +345,13 @@
         part[row : row + half] = packed(matmul(x_low, w_down[layer], NT)).astype(bf16)
     for k in range(layers - 1):
         pairs("m", k, range(k + 1, layers), w_down)
-
-    total_rows = part.shape[0]
-    piece = total_rows // (ranks * layers)
-
-    def rows(first, size):
-        return pl.ds(pl.multiple_of(first, TILE), size)
-
-    base, size, stage, starts = 0, total_rows, 0, []
-    for bit in range(bits):
-        size //= 2
-        mine = (tensor >> bit) & 1
-        keep, give = base + mine * size, base + (1 - mine) * size
-        peer = tensor ^ (1 << bit)
-        spot = total_rows - 2 * size
-        pltpu.make_async_remote_copy(
-            part.at[rows(give, size)],
-            got.at[pl.ds(spot, size)],
-            ar_s.at[stage],
-            ar_r.at[stage],
-            {"tensor": peer},
-            MESH,
-        ).start()
-        drain(got.at[pl.ds(spot, size)], ar_r.at[stage])
-        part[rows(keep, size)] = (
-            part[rows(keep, size)].astype(f32) + got[spot : spot + size].astype(f32)
-        ).astype(bf16)
-        starts.append((keep, size, peer))
-        base, stage = keep, stage + 1
-    for o, peer in enumerate(peers("section")):
-        pltpu.make_async_remote_copy(
-            part.at[rows(base + peer * piece, piece)],
-            got_y.at[o],
-            ar_s.at[stage],
-            ar_r.at[stage],
-            {"section": peer},
-            MESH,
-        ).start()
-    drain(got_y, ar_r.at[stage])
-    mine = base + section * piece
-    total = part[rows(mine, piece)].astype(f32)
-    for o in range(layers - 1):
-        total += got_y[o].astype(f32)
-    fin[rows(mine, piece)] = total.astype(bf16)
-    stage += 1
-    for peer in peers("section"):
-        pltpu.make_async_remote_copy(
-            fin.at[rows(mine, piece)],
-            fin.at[rows(mine, piece)],
-            ar_s.at[stage],
-            ar_r.at[stage],
-            {"section": peer},
-            MESH,
-        ).start()
-    drain(fin.at[pl.ds(0, (layers - 1) * piece)], ar_r.at[stage])
-    stage += 1
-    for keep, size, peer in reversed(starts):
-        pltpu.make_async_remote_copy(
-            fin.at[rows(keep, size)],
-            fin.at[rows(keep, size)],
-            ar_s.at[stage],
-            ar_r.at[stage],
-            {"tensor": peer},
-            MESH,
-        ).start()
-        drain(fin.at[pl.ds(0, size)], ar_r.at[stage])
-        stage += 1
+    for _ in range(bits):
+        advance(late_half)
+    for _ in range(2):
+        advance(early_half, late_half)
+    for _ in range(bits):
+        advance(early_half, late_half)
+    advance(late_half)
 
     def lanes(first, last=None):
         return slice(first * LANES, (first + 1 if last is None else last) * LANES)
@@ -432,15 +445,11 @@
         if layer < layers - 1:
             x = x + SCALE * matmul(zs[layer], w_up[layer], NN)
 
-    def give_back(layer, product, store, target, send, recv):
-        store[layer] = product.astype(bf16)
-
-        @pl.when(section == layer)
-        def _():
-            pltpu.make_async_copy(store.at[layer], target.at[:, columns(section)], recv).start()
-
-        @pl.when(section != layer)
-        def _():
+    def give_back(product, store, target, send, recv):
+        store[section] = product(section).astype(bf16)
+        pltpu.make_async_copy(store.at[section], target.at[:, columns(section)], recv).start()
+        for layer in peers("section"):
+            store[layer] = product(layer).astype(bf16)
             pltpu.make_async_remote_copy(
                 store.at[layer],
                 target.at[:, columns(section)],
@@ -450,31 +459,23 @@
                 MESH,
             ).start()
 
+    give_back(lambda layer: matmul(rd[layer], xs[layer], TN), back_d, grad_down, gd_s, gd_r)
     g = first_cot[...]
     for layer in reversed(range(layers)):
-        g_low = g.astype(bf16)
-        give_back(layer, SCALE * matmul(zs[layer], g_low, TN), back_u, grad_up, gu_s, gu_r)
-        give_back(layer, matmul(rd[layer], xs[layer], TN), back_d, grad_down, gd_s, gd_r)
+        gs[layer] = g.astype(bf16)
         if layer > 0:
             g = (
                 g
                 + matmul(rd[layer], w_down[layer], NN)
                 - es[layer][:, 0:1] * xs[layer].astype(f32)
             )
+    give_back(lambda layer: SCALE * matmul(zs[layer], gs[layer], TN), back_u, grad_up, gu_s, gu_r)
 
     drain(recvbuf.at[pl.ds(0, groups - 1)], tok_s)
     drain(w_down.at[pl.ds(0, layers - 1)], wd_s)
     drain(w_up.at[pl.ds(0, layers - 1)], wu_s)
-    stage = 0
-    for _, size, _ in starts:
-        drain(got.at[pl.ds(0, size)], ar_s.at[stage])
-        stage += 1
-    for _ in range(2):
-        drain(got_y, ar_s.at[stage])
-        stage += 1
-    for _, size, _ in reversed(starts):
-        drain(got.at[pl.ds(0, size)], ar_s.at[stage])
-        stage += 1
+    for first, size, sem in sent:
+        drain(fin.at[pl.ds(first, size)], sem)
     drain(back_d.at[pl.ds(0, layers - 1)], gd_s)
     drain(back_u.at[pl.ds(0, layers - 1)], gu_s)
     drain(slopes.at[pl.ds(0, groups - 1)], sl_s)
@@ -518,12 +519,12 @@
     compact = np.zeros((slots, groups * spad), np.float32)
     compact[slot_ids, slot_ids // each * spad + slot_ids % each] = 1.0
     wide = round_up(slots, LANES)
-    _, rows = payload_rows(layers, half, rank)
-    rows = round_up(rows, TILE * layers * ranks)
+    _, ends = payload_rows(layers, half, rank, TILE * layers * ranks)
+    rows = ends[-1]
     piece = rows // (layers * ranks)
     stages = 2 * (ranks.bit_length() - 1) + 2
     vmem = pl.BlockSpec(memory_space=pltpu.VMEM)
-    anywhere = pl.BlockSpec(memory_space=pl.ANY)
+    anywhere = pl.BlockSpec(memory_space=pltpu.HBM)
     b16, f32 = jnp.bfloat16, jnp.float32
     dma = pltpu.SemaphoreType.DMA
     grad_down, grad_up, slope = pl.pallas_call(
@@ -559,6 +560,7 @@
             pltpu.VMEM((layers, LANES, layers * LANES), b16),
             pltpu.VMEM((layers, LANES, layers * LANES), b16),
             pltpu.VMEM((layers, slots, fw), b16),
+            pltpu.VMEM((layers, slots, fw), b16),
             pltpu.VMEM((layers, slots, LANES), b16),
             pltpu.VMEM((layers, slots, LANES), b16),
             pltpu.VMEM((layers, slots, LANES), f32),
@@ -577,8 +579,8 @@
             dma,
             dma((layers,)),
             dma((layers,)),
-            dma((stages,)),
-            dma((stages,)),
+            dma((2, stages)),
+            dma((2, stages)),
             dma,
             dma,
             dma,

time: 125 us -> 110 us (0.88)
  Pallas kernels: 115 us -> 99.9 us
    pallas_call x1, Pallas kernels: 115 us -> 99.9 us  [on_device(): pl.pallas_call(functools.partial(kernel, cap), out_shape=(jax.ShapeDtypeS...]
where the time goes in v3:
time: 110 us; the launch traced here: 109 us
  Pallas kernels  99.9 us (91%)
  local copies, waits for them, and re-layouts  7.01 us (6%)
  other arithmetic  1.67 us (2%)
    pallas_call x1, Pallas kernels, on_device(): pl.pallas_call(functools.partial(kernel, cap), out_shape=(jax.ShapeDtypeS...  99.9 us
    unnamed x18, local copies, waits for them, and re-layouts  7.01 us

profile of v3, /device:TPU:1, one launch (start us, length us, event | category | flops | bytes accessed | tf_op | source)
XLA Modules:
  0.0 109.3 jit_solution(17304893163246444314)
XLA Ops:
  0.6 0.0 copy-start.5
  0.6 0.8 mul.17
  1.4 0.0 copy-start.6
  1.4 0.0 copy-start.7
  1.4 0.0 copy-done.5
  1.4 0.6 copy-done.6
  2.1 0.0 copy-done.7
  2.1 0.0 copy-start
  2.1 1.0 copy-done
  3.1 0.0 copy-start.1
  3.1 1.0 copy-done.1
  4.2 0.0 copy-start.2
  4.2 1.0 copy-done.2
  5.2 0.0 copy-start.3
  5.2 1.0 copy-done.3
  6.3 0.0 copy-start.4
  6.3 0.9 copy-done.4
  7.1 99.9 %shard_map.103 = (bf16[128,2048]{1,0:T(8,128)(2,1)S(1)}, bf16[128,2048]{1,0:T(8,128)(2,1)S(1)}, f32[1,128]{1,0:T(1,128)S(1)}) custom-call(s32[1,128]{1,0:T(1,128)S(1)} %bitcast.10, s32[1,128]{1,0:T(1,128)S(1)} %bitcast.11, bf16[1,2048]{1,0:T(2,128)(2,1)S(1)} %copy-done.5, bf16[128,2048]{1,0:T(8,128)(2,1)S(1)} %bitcast.8, bf16[160,256]{1,0:T(8,128)(2,1)S(1)} %copy-done.4, ...), custom_call_target="tpu_custom_call" | custom-call | tf_op jit(solution)/shard_map/pallas_call | solution.py:530
  107.1 0.9 multiply_convert_fusion
  108.0 0.8 copy.13
  108.7 0.5 copy.14
Async XLA Ops:
  0.6 0.8 copy-start.5
  1.4 0.7 copy-start.6
  1.4 0.7 copy-start.7
  2.1 1.0 copy-start
  3.1 1.0 copy-start.1
  4.2 1.0 copy-start.2
  5.2 1.0 copy-start.3
  6.3 0.9 copy-start.4

commit v4 on v3

--- a/solution.py
+++ b/solution.py
@@ -3,7 +3,6 @@
 
 import jax
 import jax.numpy as jnp
-import numpy as np
 from jax import lax
 from jax.experimental import pallas as pl
 from jax.experimental.pallas import tpu as pltpu
@@ -58,7 +57,6 @@
     choose,
     gains,
     down,
-    compact,
     tokens,
     cotangent,
     up,
@@ -69,11 +67,12 @@
     choose_v,
     gains_v,
     down_v,
-    compact_v,
     tokv,
     cotv,
     sendbuf,
     recvbuf,
+    gains_wide,
+    w_gain,
     down_scaled,
     w_down,
     w_up,
@@ -105,8 +104,10 @@
     tok_r,
     wd_s,
     wu_s,
+    wg_s,
     wd_r,
     wu_r,
+    wg_r,
     ar_s,
     ar_r,
     gd_s,
@@ -154,7 +155,6 @@
                 (cotangent.at[:, columns(section)], cotv),
                 (gains, gains_v),
                 (down, down_v),
-                (compact, compact_v),
             )
         )
     ]
@@ -182,6 +182,8 @@
         load.wait()
     down_scaled[...] = (down_v[...].astype(f32) * gains_v[...].astype(f32)).astype(bf16)
     spread(down_scaled, w_down, wd_s, wd_r)
+    gains_wide[...] = jnp.broadcast_to(gains_v[...], gains_wide.shape)
+    spread(gains_wide, w_gain, wg_s, wg_r)
 
     early = lax.broadcasted_iota(jnp.int32, (count, count), 0)
     late = lax.broadcasted_iota(jnp.int32, (count, count), 1)
@@ -218,8 +220,14 @@
         ).start()
     recvbuf[dp] = sendbuf[dp]
 
+    cell = lax.broadcasted_iota(jnp.int32, (1, groups * spad), 1)
+    source = sum((cell >= d * spad).astype(jnp.int32) for d in range(1, groups))
+    within = cell - source * spad
+    wanted = jnp.where(within < each, source * each + within, -1)
+    slot_ids = lax.broadcasted_iota(jnp.int32, (slots, groups * spad), 0)
+    compact = jnp.where(slot_ids == wanted, 1.0, 0.0).astype(bf16)
     drain(recvbuf.at[pl.ds(0, groups - 1)], tok_r)
-    arrived = matmul(compact_v[...], recvbuf[...].reshape(groups * spad, 2 * fw + LANES), NN)
+    arrived = matmul(compact, recvbuf[...].reshape(groups * spad, 2 * fw + LANES), NN)
     x0 = arrived[:, 0:fw]
     first_x[...] = x0
     first_cot[...] = arrived[:, fw : 2 * fw]
@@ -459,7 +467,15 @@
                 MESH,
             ).start()
 
-    give_back(lambda layer: matmul(rd[layer], xs[layer], TN), back_d, grad_down, gd_s, gd_r)
+    for layer in range(layers):
+        drain(w_gain.at[layer], wg_r.at[layer])
+    give_back(
+        lambda layer: matmul(rd[layer], xs[layer], TN) * w_gain[layer, 0:1].astype(f32),
+        back_d,
+        grad_down,
+        gd_s,
+        gd_r,
+    )
     g = first_cot[...]
     for layer in reversed(range(layers)):
         gs[layer] = g.astype(bf16)
@@ -474,6 +490,7 @@
     drain(recvbuf.at[pl.ds(0, groups - 1)], tok_s)
     drain(w_down.at[pl.ds(0, layers - 1)], wd_s)
     drain(w_up.at[pl.ds(0, layers - 1)], wu_s)
+    drain(w_gain.at[pl.ds(0, layers - 1)], wg_s)
     for first, size, sem in sent:
         drain(fin.at[pl.ds(first, size)], sem)
     drain(back_d.at[pl.ds(0, layers - 1)], gd_s)
@@ -493,6 +510,31 @@
 
     drain(grad_up, gu_r)
     drain(grad_down, gd_r)
+
+
+def finish(raw_down, raw_up, raw_slope, grad_down, grad_up, slope, v_down, v_up, v_slope, loads, stores):
+    parts = (loads.shape[0] - 1) // 2
+    rows = grad_up.shape[0] // parts
+    pieces = [(raw_slope, v_slope, slope)]
+    for i in range(parts):
+        some = pl.ds(i * rows, rows)
+        pieces.append((raw_up.at[some], v_up.at[some], grad_up.at[some]))
+        pieces.append((raw_down.at[some], v_down.at[some], grad_down.at[some]))
+    reads = [
+        pltpu.make_async_copy(source, through, loads.at[i])
+        for i, (source, through, _) in enumerate(pieces)
+    ]
+    writes = [
+        pltpu.make_async_copy(through, target, stores.at[i])
+        for i, (_, through, target) in enumerate(pieces)
+    ]
+    for read in reads:
+        read.start()
+    for read, write in zip(reads, writes):
+        read.wait()
+        write.start()
+    for write in writes:
+        write.wait()
 
 
 def on_device(
@@ -515,9 +557,6 @@
     adapters, rank = adapter_down_weights.shape[1:3]
     weight_rows = adapters * rank
     half = slots // 2
-    slot_ids = np.arange(slots)
-    compact = np.zeros((slots, groups * spad), np.float32)
-    compact[slot_ids, slot_ids // each * spad + slot_ids % each] = 1.0
     wide = round_up(slots, LANES)
     _, ends = payload_rows(layers, half, rank, TILE * layers * ranks)
     rows = ends[-1]
@@ -527,25 +566,26 @@
     anywhere = pl.BlockSpec(memory_space=pltpu.HBM)
     b16, f32 = jnp.bfloat16, jnp.float32
     dma = pltpu.SemaphoreType.DMA
-    grad_down, grad_up, slope = pl.pallas_call(
+    raw = pl.pallas_call(
         functools.partial(kernel, cap),
         out_shape=(
             jax.ShapeDtypeStruct((weight_rows, local), b16),
             jax.ShapeDtypeStruct((weight_rows, local), b16),
             jax.ShapeDtypeStruct((1, count), f32),
         ),
-        in_specs=[anywhere] * 8,
-        out_specs=(vmem, vmem, vmem),
+        in_specs=[anywhere] * 7,
+        out_specs=(anywhere, anywhere, vmem),
         scratch_shapes=[
             pltpu.VMEM((1, count), jnp.int32),
             pltpu.VMEM((1, count), jnp.int32),
             pltpu.VMEM((1, local), b16),
             pltpu.VMEM((weight_rows, local), b16),
-            pltpu.VMEM(compact.shape, b16),
             pltpu.VMEM((count, fw), b16),
             pltpu.VMEM((count, fw), b16),
             pltpu.VMEM((groups, spad, 2 * fw + LANES), b16),
             pltpu.VMEM((groups, spad, 2 * fw + LANES), b16),
+            pltpu.VMEM((TILE, local), b16),
+            pltpu.VMEM((layers, TILE, fw), b16),
             pltpu.VMEM((weight_rows, local), b16),
             pltpu.VMEM((layers, weight_rows, fw), b16),
             pltpu.VMEM((layers, weight_rows, fw), b16),
@@ -572,11 +612,13 @@
             pltpu.VMEM((layers, weight_rows, fw), b16),
             pltpu.VMEM((8, wide), f32),
             pltpu.VMEM((groups, 8, wide), f32),
-            dma((7,)),
-            dma,
-            dma,
-            dma,
-            dma,
+            dma((6,)),
+            dma,
+            dma,
+            dma,
+            dma,
+            dma,
+            dma((layers,)),
             dma((layers,)),
             dma((layers,)),
             dma((2, stages)),
@@ -589,19 +631,25 @@
             dma,
         ],
         compiler_params=pltpu.CompilerParams(
-            collective_id=0, has_side_effects=True, vmem_limit_bytes=48 * 1024 * 1024
+            collective_id=0, has_side_effects=True, vmem_limit_bytes=62 * 1024 * 1024
         ),
     )(
         owner_indices.reshape(1, count),
         local_adapter_index.reshape(1, count),
         gains,
         adapter_down_weights.reshape(weight_rows, local),
-        jnp.asarray(compact, b16),
         tokens,
         cotangent,
         adapter_up_weights.reshape(weight_rows, local),
     )
-    grad_down = (grad_down.astype(f32) * gains.astype(f32)).astype(b16)
+    grad_down, grad_up, slope = pl.pallas_call(
+        finish,
+        out_shape=tuple(jax.ShapeDtypeStruct(r.shape, r.dtype) for r in raw),
+        in_specs=[anywhere] * 3,
+        out_specs=(anywhere,) * 3,
+        scratch_shapes=[pltpu.VMEM(r.shape, r.dtype) for r in raw] + [dma((9,)), dma((9,))],
+        compiler_params=pltpu.CompilerParams(vmem_limit_bytes=62 * 1024 * 1024),
+    )(*raw)
     shape = (1, adapters, rank, local)
     return (grad_down.reshape(shape), grad_up.reshape(shape), slope)
 

time: 110 us -> 104 us (0.945)
  local copies, waits for them, and re-layouts: 7.01 us -> 0 us
  Pallas kernels: 99.9 us -> 103 us
  other arithmetic: 1.67 us -> 0 us
    unnamed x18 -> x0, local copies, waits for them, and re-layouts: 7.01 us -> none
    pallas_call x0 -> x1, Pallas kernels: none -> 2.11 us  [on_device(): pl.pallas_call(finish, out_shape=tuple((jax.ShapeDtypeStruct(r.shape, r.d...]
where the time goes in v4:
time: 104 us; the launch traced here: 103 us
  Pallas kernels  103 us (99%)
    pallas_call x1, Pallas kernels, on_device(): pl.pallas_call(functools.partial(kernel, cap), out_shape=(jax.ShapeDtypeS...  101 us
    pallas_call x1, Pallas kernels, on_device(): pl.pallas_call(finish, out_shape=tuple((jax.ShapeDtypeStruct(r.shape, r.d...  2.11 us

profile of v4, /device:TPU:1, one launch (start us, length us, event | category | flops | bytes accessed | tf_op | source)
XLA Modules:
  0.0 103.4 jit_solution(8806945604668865986)
XLA Ops:
  0.6 100.7 %shard_map.94 = (bf16[128,2048]{1,0:T(8,128)(2,1)}, bf16[128,2048]{1,0:T(8,128)(2,1)}, f32[1,128]{1,0:T(1,128)}) custom-call(s32[1,128]{1,0:T(1,128)} %bitcast.8, s32[1,128]{1,0:T(1,128)} %bitcast.9, bf16[1,2048]{1,0:T(2,128)(2,1)} %gains.1, bf16[128,2048]{1,0:T(8,128)(2,1)} %bitcast.6, bf16[128,2048]{1,0:T(8,128)(2,1)} %tokens.1, ...), custom_call_target="tpu_custom_call" | custom-call | tf_op jit(solution)/shard_map/pallas_call | solution.py:569
  101.3 2.1 %shard_map.95 = (bf16[128,2048]{1,0:T(8,128)(2,1)}, bf16[128,2048]{1,0:T(8,128)(2,1)}, f32[1,128]{1,0:T(1,128)}) custom-call(bf16[128,2048]{1,0:T(8,128)(2,1)} %get-tuple-element.9.raw_down, bf16[128,2048]{1,0:T(8,128)(2,1)} %get-tuple-element.10.raw_up, f32[1,128]{1,0:T(1,128)} %get-tuple-element.11.raw_slope), custom_call_target="tpu_custom_call" | custom-call | tf_op jit(solution)/shard_map/pallas_call | solution.py:645

commit v5 on v4

--- a/solution.py
+++ b/solution.py
@@ -11,6 +11,7 @@
 MTOK = 64
 LANES = 128
 TILE = 16
+JOINT = True
 EPS = 1e-05
 SCALE = 0.5
 MESH = pl.DeviceIdType.MESH
@@ -33,19 +34,25 @@
 
 def peers(axis):
     count, me = lax.axis_size(axis), lax.axis_index(axis)
-    return [lax.rem(me + o, count) for o in range(1, count)]
+    offsets = sorted(range(1, count), key=lambda o: (-min(o, count - o), o))
+    return [lax.rem(me + o, count) for o in offsets]
 
 
 def payload_rows(layers, half, rank, unit):
     at, ends = {}, []
     at["squares"], rows = 0, TILE
-    for number, name, count in (("u", "q", layers - 1), ("m", "p", layers)):
+    for name, count in (("q", layers - 1), ("r", layers)):
         at[name], rows = rows, rows + count * half
-        if number == "u":
-            at["r"], rows = rows, rows + layers * half
+    for k in range(layers - 1):
+        for other in range(k, layers - 1):
+            at["u", k, other], rows = rows, rows + rank
+    rows = round_up(rows, unit)
+    ends.append(rows)
+    for part in range(2):
+        at["p", part], rows = rows, rows + layers // 2 * half
         for k in range(layers - 1):
-            for other in range(k, layers - 1) if number == "u" else range(k + 1, layers):
-                at[number, k, other], rows = rows, rows + rank
+            for pair in range((k + 1) // 2, layers // 2):
+                at["m", part, k, pair], rows = rows, rows + rank
         rows = round_up(rows, unit)
         ends.append(rows)
     return at, ends
@@ -66,6 +73,7 @@
     own_v,
     choose_v,
     gains_v,
+    up_v,
     down_v,
     tokv,
     cotv,
@@ -90,8 +98,8 @@
     gs,
     zs,
     rd,
-    es,
     prods,
+    cur,
     first_x,
     first_cot,
     mask,
@@ -137,25 +145,34 @@
 
     barrier = pltpu.get_barrier_semaphore()
     greeted = 0
-    for axis in ("tensor", "section", "dp"):
-        for peer in peers(axis):
-            pl.semaphore_signal(barrier, inc=1, device_id={axis: peer}, device_id_type=MESH)
-            greeted += 1
+    greet = [{axis: peer} for axis in ("tensor", "section", "dp") for peer in peers(axis)]
+    if bits > 1:
+        greet += [{"tensor": tensor ^ 2, "section": peer} for peer in peers("section")]
+    for device in greet:
+        pl.semaphore_signal(barrier, inc=1, device_id=device, device_id_type=MESH)
+        greeted += 1
 
     def columns(index):
         return pl.ds(pl.multiple_of(index * fw, LANES), fw)
 
+    quarter = rank // 2
+    blocks = [
+        (pl.ds((2 * a + h) * quarter, quarter), pl.ds((2 * h + a) * quarter, quarter))
+        for a in range(2)
+        for h in range(2)
+    ]
     loads = [
         pltpu.make_async_copy(source, target, loc_sem.at[i])
         for i, (source, target) in enumerate(
-            (
+            [
                 (own, own_v),
                 (choose, choose_v),
                 (tokens.at[:, columns(section)], tokv),
                 (cotangent.at[:, columns(section)], cotv),
                 (gains, gains_v),
-                (down, down_v),
-            )
+            ]
+            + [(up.at[there], up_v.at[here]) for there, here in blocks]
+            + [(down.at[there], down_v.at[here]) for there, here in blocks]
         )
     ]
     for load in loads:
@@ -163,25 +180,37 @@
 
     pl.semaphore_wait(barrier, greeted)
 
-    def spread(source, target, send, recv):
+    def spread(source, target, send, recv, some=None):
+        def rows_of(ref):
+            return ref if some is None else ref.at[some]
+
         for peer in peers("section"):
             pltpu.make_async_remote_copy(
-                source.at[:, columns(peer)],
-                target.at[section],
+                rows_of(source).at[:, columns(peer)],
+                rows_of(target.at[section]),
                 send,
                 recv.at[section],
                 {"section": peer},
                 MESH,
             ).start()
         pltpu.make_async_copy(
-            source.at[:, columns(section)], target.at[section], recv.at[section]
+            rows_of(source).at[:, columns(section)], rows_of(target.at[section]), recv.at[section]
         ).start()
 
-    spread(up, w_up, wu_s, wu_r)
-    for load in loads[4:]:
+    for load in loads[5:9]:
+        load.wait()
+    spread(up_v, w_up, wu_s, wu_r)
+    for load in loads[4:5] + loads[9:]:
         load.wait()
     down_scaled[...] = (down_v[...].astype(f32) * gains_v[...].astype(f32)).astype(bf16)
-    spread(down_scaled, w_down, wd_s, wd_r)
+    for part_of in range(2):
+        spread(
+            down_scaled,
+            w_down,
+            wd_s,
+            wd_r.at[part_of],
+            pl.ds(part_of * rank, rank),
+        )
     gains_wide[...] = jnp.broadcast_to(gains_v[...], gains_wide.shape)
     spread(gains_wide, w_gain, wg_s, wg_r)
 
@@ -233,21 +262,47 @@
     first_cot[...] = arrived[:, fw : 2 * fw]
     lane = lax.broadcasted_iota(jnp.int32, (slots, LANES), 1)
     second = arrived[:, 2 * fw :] > 0.5
-    mask[...] = jnp.where(second == (lane >= rank), 1.0, 0.0)
-
-    low = lax.broadcasted_iota(jnp.int32, (half, LANES), 1) < rank
-    low_rank = lax.broadcasted_iota(jnp.int32, (rank, LANES), 1) < rank
+    mask[...] = jnp.where(second == ((lane & quarter) > 0), 1.0, 0.0)
+
+    even = (lax.broadcasted_iota(jnp.int32, (half, LANES), 1) & quarter) == 0
+    even_rank = (lax.broadcasted_iota(jnp.int32, (rank, LANES), 1) & quarter) == 0
+    left = lane < rank
+    left_rank = lax.broadcasted_iota(jnp.int32, (rank, LANES), 1) < rank
     tall = lax.broadcasted_iota(jnp.int32, (TILE, LANES), 1)
 
     def packed(total):
         kept = total * mask[...]
-        both = kept + pltpu.roll(kept, rank, 1)
-        return jnp.where(low, both[0:half], both[half:])
+        first = kept[0:half] + pltpu.roll(kept[0:half], LANES - quarter, 1)
+        last = kept[half:] + pltpu.roll(kept[half:], quarter, 1)
+        return jnp.where(even, first, last).astype(bf16)
 
     def unpacked(total):
-        turned = pltpu.roll(total, rank, 1)
-        both = jnp.concatenate([jnp.where(low, total, turned), jnp.where(low, turned, total)], 0)
-        return both * mask[...]
+        total = total.astype(f32)
+        first = jnp.where(even, total, pltpu.roll(total, quarter, 1))
+        last = jnp.where(even, pltpu.roll(total, LANES - quarter, 1), total)
+        return jnp.concatenate([first, last], 0) * mask[...]
+
+    def thinned(block):
+        first, second, third, fourth = (
+            block[i * quarter : (i + 1) * quarter] for i in range(4)
+        )
+        return jnp.where(
+            even_rank,
+            jnp.concatenate([first, third], 0),
+            jnp.concatenate([second, fourth], 0),
+        ).astype(bf16)
+
+    def widened(block):
+        block = block.astype(f32)
+        evens, odds = jnp.where(even_rank, block, 0.0), jnp.where(even_rank, 0.0, block)
+        return jnp.concatenate(
+            [evens[0:quarter], odds[0:quarter], evens[quarter:], odds[quarter:]], 0
+        ).astype(bf16)
+
+    def layer_of(first, last, which, keep_left):
+        if which == 0:
+            return jnp.where(keep_left, first, pltpu.roll(last, rank, 1))
+        return jnp.where(keep_left, pltpu.roll(first, rank, 1), last)
 
     squares = jnp.sum(x0 * x0, 1, keepdims=True)
     folded = jnp.zeros((TILE, LANES), f32)
@@ -263,38 +318,63 @@
         weight = w_up[layer]
         if layer < layers - 1:
             row = at["q"] + layer * half
-            part[row : row + half] = packed(matmul(x_low, weight, NT)).astype(bf16)
+            part[row : row + half] = packed(matmul(x_low, weight, NT))
         row = at["r"] + layer * half
-        part[row : row + half] = packed(matmul(cot_low, weight, NT)).astype(bf16)
-
-    def pairs(name, k, others, weights):
-        first, last = others[0], others[-1] + 1
-        stacked = weights[first:last].reshape((last - first) * LANES, fw)
+        part[row : row + half] = packed(matmul(cot_low, weight, NT))
+    for k in range(layers - 1):
+        stacked = w_up[k : layers - 1].reshape((layers - 1 - k) * LANES, fw)
         product = matmul(w_up[k], stacked, NT)
-        for i, other in enumerate(others):
-            block = product[:, i * LANES : (i + 1) * LANES]
-            row = at[name, k, other]
-            part[row : row + rank] = jnp.where(low_rank, block[0:rank], block[rank:]).astype(bf16)
-
-    for k in range(layers - 1):
-        pairs("u", k, range(k, layers - 1), w_up)
+        for i, other in enumerate(range(k, layers - 1)):
+            row = at["u", k, other]
+            part[row : row + rank] = thinned(product[:, i * LANES : (i + 1) * LANES])
+
+    def down_products(h):
+        for layer in range(layers):
+            drain(w_down.at[layer, pl.ds(h * rank, rank)], wd_r.at[h, layer])
+        weights = w_down[:, h * rank : (h + 1) * rank].reshape(layers * rank, fw)
+        product = matmul(x_low, weights, NT)
+        for pair in range(layers // 2):
+            row = at["p", h] + pair * half
+            part[row : row + half] = packed(product[:, pair * LANES : (pair + 1) * LANES])
+        for k in range(layers - 1):
+            skip = (k + 1) // 2
+            product = matmul(w_up[k], weights[skip * LANES :], NT)
+            for pair in range(skip, layers // 2):
+                row = at["m", h, k, pair]
+                i = pair - skip
+                part[row : row + rank] = thinned(product[:, i * LANES : (i + 1) * LANES])
 
     def rows(first, size):
         return pl.ds(pl.multiple_of(first, TILE), size)
 
-    def all_reduce(chunk):
+    def all_reduce(chunk, joint):
         first = ends[chunk - 1] if chunk else 0
         size = ends[chunk] - first
-        whole, piece, y_first = size, size // (ranks * layers), first // (ranks * layers)
+        halvings = bits - 1 if joint and bits > 1 else bits
+        strides = [] if halvings == bits else [1 << halvings]
+        whole, piece = size, (size >> halvings) // (layers << len(strides))
         base, stage, starts = first, 0, []
         sends, arrivals = ar_s.at[chunk], ar_r.at[chunk]
+        others = [({"section": peer}, peer, 0) for peer in peers("section")]
+        high = 0
+        for stride in strides:
+            high = (tensor // stride) & 1
+            away = tensor ^ stride
+            others = (
+                [({"section": peer, "tensor": away}, peer, 1) for peer in peers("section")]
+                + others
+                + [({"tensor": away}, section, 1)]
+            )
+
+        def index_of(peer, crossed):
+            return peer + layers * (high + crossed - 2 * high * crossed)
 
         def send(source, target, device):
             pltpu.make_async_remote_copy(
                 source, target, sends.at[stage], arrivals.at[stage], device, MESH
             ).start()
 
-        for bit in range(bits):
+        for bit in range(halvings):
             size //= 2
             mine = (tensor >> bit) & 1
             keep, give = base + mine * size, base + (1 - mine) * size
@@ -308,24 +388,26 @@
             ).astype(bf16)
             starts.append((keep, size, peer))
             base, stage = keep, stage + 1
-        for o, peer in enumerate(peers("section")):
+        landed = got_y.at[chunk]
+        for o, (device, peer, crossed) in enumerate(others):
             send(
-                part.at[rows(base + peer * piece, piece)],
-                got_y.at[o, pl.ds(y_first, piece)],
-                {"section": peer},
+                part.at[rows(base + index_of(peer, crossed) * piece, piece)],
+                landed.at[pl.ds(o * piece, piece)],
+                device,
             )
         yield
-        drain(fin.at[pl.ds(first, (layers - 1) * piece)], arrivals.at[stage])
+        filled = len(others) * piece
+        drain(landed.at[pl.ds(0, filled)], arrivals.at[stage])
         stage += 1
-        mine = base + section * piece
+        mine = base + index_of(section, 0) * piece
         total = part[rows(mine, piece)].astype(f32)
-        for o in range(layers - 1):
-            total += got_y[o, y_first : y_first + piece].astype(f32)
+        for o in range(len(others)):
+            total += got_y[chunk, o * piece : (o + 1) * piece].astype(f32)
         fin[rows(mine, piece)] = total.astype(bf16)
-        for peer in peers("section"):
-            send(fin.at[rows(mine, piece)], fin.at[rows(mine, piece)], {"section": peer})
+        for device, _, _ in others:
+            send(fin.at[rows(mine, piece)], fin.at[rows(mine, piece)], device)
         yield
-        drain(fin.at[pl.ds(first, (layers - 1) * piece)], arrivals.at[stage])
+        drain(fin.at[pl.ds(first, filled)], arrivals.at[stage])
         stage += 1
         for keep, size, peer in reversed(starts):
             send(fin.at[rows(keep, size)], fin.at[rows(keep, size)], {"tensor": peer})
@@ -333,56 +415,50 @@
             drain(fin.at[pl.ds(first, size)], arrivals.at[stage])
             stage += 1
         sizes = [size for _, size, _ in starts]
-        y_size = (layers - 1) * piece
-        for i, size in enumerate([*sizes, y_size, y_size, *reversed(sizes)]):
+        for i, size in enumerate([*sizes, filled, filled, *reversed(sizes)]):
             sent.append((first, size, sends.at[i]))
 
     sent = []
-    early_half, late_half = all_reduce(0), all_reduce(1)
-
-    def advance(*halves):
-        for chunk in halves:
-            next(chunk, None)
-
-    for _ in range(bits + 1):
-        advance(early_half)
-    for layer in range(layers):
-        drain(w_down.at[layer], wd_r.at[layer])
-    for layer in range(layers):
-        row = at["p"] + layer * half
-        part[row : row + half] = packed(matmul(x_low, w_down[layer], NT)).astype(bf16)
-    for k in range(layers - 1):
-        pairs("m", k, range(k + 1, layers), w_down)
-    for _ in range(bits):
-        advance(late_half)
-    for _ in range(2):
-        advance(early_half, late_half)
-    for _ in range(bits):
-        advance(early_half, late_half)
-    advance(late_half)
+    chunks = [all_reduce(0, False), all_reduce(1, False), all_reduce(2, JOINT)]
+
+    def advance(order):
+        for chunk in order:
+            next(chunks[chunk], None)
+
+    advance([0, 0])
+    down_products(0)
+    advance([1])
+    advance([0, 1] if bits > 1 else [1])
+    down_products(1)
+    advance([2])
+    advance([1, 2, 0, 1, 2, 0, 1, 2, 0, 1, 2, 0, 1, 2, 0, 1, 2])
 
     def lanes(first, last=None):
         return slice(first * LANES, (first + 1 if last is None else last) * LANES)
 
-    for name, target, number in (
-        ("p", acc_p, layers),
-        ("q", acc_q, layers - 1),
-        ("r", acc_w, layers),
-    ):
+    for name, target, number in (("q", acc_q, layers - 1), ("r", acc_w, layers)):
         for layer in range(number):
             row = at[name] + layer * half
-            target[:, lanes(layer)] = unpacked(fin[row : row + half].astype(f32))
+            target[:, lanes(layer)] = unpacked(fin[row : row + half])
+    for pair in range(layers // 2):
+        row, last_row = (at["p", h] + pair * half for h in range(2))
+        first = unpacked(fin[row : row + half])
+        last = unpacked(fin[last_row : last_row + half])
+        for which in range(2):
+            acc_p[:, lanes(2 * pair + which)] = layer_of(first, last, which, left)
     for k in range(layers - 1):
-        for name, target, others in (
-            ("m", big_m, range(k + 1, layers)),
-            ("u", big_u, range(k, layers - 1)),
-        ):
-            for other in others:
-                row = at[name, k, other]
-                block = fin[row : row + rank]
-                zero = jnp.zeros_like(block)
-                target[k, 0:rank, lanes(other)] = jnp.where(low_rank, block, zero)
-                target[k, rank:, lanes(other)] = jnp.where(low_rank, zero, block)
+        for other in range(k, layers - 1):
+            row = at["u", k, other]
+            big_u[k, :, lanes(other)] = widened(fin[row : row + rank])
+        for pair in range((k + 1) // 2, layers // 2):
+            first, last = (
+                fin[row : row + rank].astype(f32)
+                for row in (at["m", h, k, pair] for h in range(2))
+            )
+            for which in range(2):
+                if 2 * pair + which > k:
+                    block = layer_of(first, last, which, left_rank)
+                    big_m[k, :, lanes(2 * pair + which)] = widened(block)
     folded = fin[0:TILE].astype(f32)
     squares = jnp.concatenate(
         [
@@ -398,9 +474,10 @@
         scales.append(scale_rows)
         latent = (acc_p[:, lanes(k)] * scale_rows).astype(bf16)
         zs[k] = latent
-        if k == layers - 1:
-            break
+        x = first_x[...] if k == 0 else cur[...]
+        xs[k] = x.astype(bf16)
         if k < layers - 1:
+            cur[...] = x + SCALE * matmul(latent, w_up[k], NN)
             acc_p[:, lanes(k + 1, layers)] += SCALE * matmul(
                 latent, big_m[k, :, lanes(k + 1, layers)], NN
             )
@@ -426,13 +503,39 @@
         scale_rows = scales[m]
         scaled = (rank_low.astype(f32) * scale_rows).astype(bf16)
         rd[m] = scaled
+        g = first_cot[...] if m == layers - 1 else cur[...]
+        gs[m] = g.astype(bf16)
         if m > 0:
             weight = scale_rows * scale_rows * jnp.sum(product, 1, keepdims=True) / width
-            es[m] = jnp.broadcast_to(weight, (slots, LANES))
+            cur[...] = (
+                g + matmul(scaled, w_down[m], NN) - weight * xs[m].astype(f32)
+            )
             others = big_m[0:m, :, lanes(m)].reshape(m * LANES, LANES)
             acc_w[:, lanes(0, m)] += matmul(scaled, others, NT) - weight * seen[
                 m, :, lanes(0, m)
             ].astype(f32)
+
+    for layer in range(layers):
+        drain(w_gain.at[layer], wg_r.at[layer])
+
+    def down_grad(layer):
+        gain = w_gain[layer, 0:1].astype(f32)
+        back_d[layer] = (matmul(rd[layer], xs[layer], TN) * gain).astype(bf16)
+        return back_d.at[layer], grad_down.at[:, columns(section)], gd_s, gd_r
+
+    def up_grad(layer):
+        back_u[layer] = (SCALE * matmul(zs[layer], gs[layer], TN)).astype(bf16)
+        return back_u.at[layer], grad_up.at[:, columns(section)], gu_s, gu_r
+
+    for make in (down_grad, up_grad):
+        for layer in peers("section"):
+            source, target, send, recv = make(layer)
+            pltpu.make_async_remote_copy(
+                source, target, send, recv, {"section": layer}, MESH
+            ).start()
+    for make in (down_grad, up_grad):
+        source, target, _, recv = make(section)
+        pltpu.make_async_copy(source, target, recv).start()
 
     slope_row[:, 0:slots] = lax.dot_general(
         jnp.full((8, LANES), 1.0 / math.sqrt(width), f32),
@@ -447,46 +550,6 @@
         ).start()
     slopes[dp] = slope_row[...]
 
-    x = first_x[...]
-    for layer in range(layers):
-        xs[layer] = x.astype(bf16)
-        if layer < layers - 1:
-            x = x + SCALE * matmul(zs[layer], w_up[layer], NN)
-
-    def give_back(product, store, target, send, recv):
-        store[section] = product(section).astype(bf16)
-        pltpu.make_async_copy(store.at[section], target.at[:, columns(section)], recv).start()
-        for layer in peers("section"):
-            store[layer] = product(layer).astype(bf16)
-            pltpu.make_async_remote_copy(
-                store.at[layer],
-                target.at[:, columns(section)],
-                send,
-                recv,
-                {"section": layer},
-                MESH,
-            ).start()
-
-    for layer in range(layers):
-        drain(w_gain.at[layer], wg_r.at[layer])
-    give_back(
-        lambda layer: matmul(rd[layer], xs[layer], TN) * w_gain[layer, 0:1].astype(f32),
-        back_d,
-        grad_down,
-        gd_s,
-        gd_r,
-    )
-    g = first_cot[...]
-    for layer in reversed(range(layers)):
-        gs[layer] = g.astype(bf16)
-        if layer > 0:
-            g = (
-                g
-                + matmul(rd[layer], w_down[layer], NN)
-                - es[layer][:, 0:1] * xs[layer].astype(f32)
-            )
-    give_back(lambda layer: SCALE * matmul(zs[layer], gs[layer], TN), back_u, grad_up, gu_s, gu_r)
-
     drain(recvbuf.at[pl.ds(0, groups - 1)], tok_s)
     drain(w_down.at[pl.ds(0, layers - 1)], wd_s)
     drain(w_up.at[pl.ds(0, layers - 1)], wu_s)
@@ -516,10 +579,10 @@
     parts = (loads.shape[0] - 1) // 2
     rows = grad_up.shape[0] // parts
     pieces = [(raw_slope, v_slope, slope)]
-    for i in range(parts):
-        some = pl.ds(i * rows, rows)
-        pieces.append((raw_up.at[some], v_up.at[some], grad_up.at[some]))
-        pieces.append((raw_down.at[some], v_down.at[some], grad_down.at[some]))
+    for i, block in enumerate((0, 2, 1, 3)):
+        some, home = pl.ds(i * rows, rows), pl.ds(block * rows, rows)
+        pieces.append((raw_up.at[some], v_up.at[some], grad_up.at[home]))
+        pieces.append((raw_down.at[some], v_down.at[some], grad_down.at[home]))
     reads = [
         pltpu.make_async_copy(source, through, loads.at[i])
         for i, (source, through, _) in enumerate(pieces)
@@ -560,7 +623,7 @@
     wide = round_up(slots, LANES)
     _, ends = payload_rows(layers, half, rank, TILE * layers * ranks)
     rows = ends[-1]
-    piece = rows // (layers * ranks)
+    most = max(b - a for a, b in zip([0] + ends, ends))
     stages = 2 * (ranks.bit_length() - 1) + 2
     vmem = pl.BlockSpec(memory_space=pltpu.VMEM)
     anywhere = pl.BlockSpec(memory_space=pltpu.HBM)
@@ -580,6 +643,7 @@
             pltpu.VMEM((1, count), jnp.int32),
             pltpu.VMEM((1, local), b16),
             pltpu.VMEM((weight_rows, local), b16),
+            pltpu.VMEM((weight_rows, local), b16),
             pltpu.VMEM((count, fw), b16),
             pltpu.VMEM((count, fw), b16),
             pltpu.VMEM((groups, spad, 2 * fw + LANES), b16),
@@ -592,7 +656,7 @@
             pltpu.VMEM((rows, LANES), b16),
             pltpu.VMEM((rows, LANES), b16),
             pltpu.VMEM((rows, LANES), b16),
-            pltpu.VMEM((layers - 1, piece, LANES), b16),
+            pltpu.VMEM((3, most, LANES), b16),
             pltpu.VMEM((slots, layers * LANES), f32),
             pltpu.VMEM((slots, layers * LANES), f32),
             pltpu.VMEM((slots, layers * LANES), f32),
@@ -604,7 +668,7 @@
             pltpu.VMEM((layers, slots, LANES), b16),
             pltpu.VMEM((layers, slots, LANES), b16),
             pltpu.VMEM((layers, slots, LANES), f32),
-            pltpu.VMEM((layers, slots, LANES), f32),
+            pltpu.VMEM((slots, fw), f32),
             pltpu.VMEM((slots, fw), f32),
             pltpu.VMEM((slots, fw), f32),
             pltpu.VMEM((slots, LANES), f32),
@@ -612,17 +676,17 @@
             pltpu.VMEM((layers, weight_rows, fw), b16),
             pltpu.VMEM((8, wide), f32),
             pltpu.VMEM((groups, 8, wide), f32),
-            dma((6,)),
-            dma,
-            dma,
-            dma,
-            dma,
-            dma,
+            dma((13,)),
+            dma,
+            dma,
+            dma,
+            dma,
+            dma,
+            dma((2, layers)),
             dma((layers,)),
             dma((layers,)),
-            dma((layers,)),
-            dma((2, stages)),
-            dma((2, stages)),
+            dma((3, stages)),
+            dma((3, stages)),
             dma,
             dma,
             dma,

time: 104 us -> 100 us (0.962)
  Pallas kernels: 103 us -> 99.6 us
    pallas_call x1, Pallas kernels: 101 us -> 97.4 us  [on_device(): pl.pallas_call(functools.partial(kernel, cap), out_shape=(jax.ShapeDtypeS...]
where the time goes in v5:
time: 100 us
  Pallas kernels  99.6 us (100%)
    pallas_call x1, Pallas kernels, on_device(): pl.pallas_call(functools.partial(kernel, cap), out_shape=(jax.ShapeDtypeS...  97.4 us
    pallas_call x1, Pallas kernels, on_device(): pl.pallas_call(finish, out_shape=tuple((jax.ShapeDtypeStruct(r.shape, r.d...  2.11 us

profile of v5, /device:TPU:1, one launch (start us, length us, event | category | flops | bytes accessed | tf_op | source)
XLA Modules:
  0.0 100.2 jit_solution(13562191232310205246)
XLA Ops:
  0.6 97.4 %shard_map.94 = (bf16[128,2048]{1,0:T(8,128)(2,1)}, bf16[128,2048]{1,0:T(8,128)(2,1)}, f32[1,128]{1,0:T(1,128)}) custom-call(s32[1,128]{1,0:T(1,128)} %bitcast.8, s32[1,128]{1,0:T(1,128)} %bitcast.9, bf16[1,2048]{1,0:T(2,128)(2,1)} %gains.1, bf16[128,2048]{1,0:T(8,128)(2,1)} %bitcast.6, bf16[128,2048]{1,0:T(8,128)(2,1)} %tokens.1, ...), custom_call_target="tpu_custom_call" | custom-call | tf_op jit(solution)/shard_map/pallas_call | solution.py:632
  98.1 2.1 %shard_map.95 = (bf16[128,2048]{1,0:T(8,128)(2,1)}, bf16[128,2048]{1,0:T(8,128)(2,1)}, f32[1,128]{1,0:T(1,128)}) custom-call(bf16[128,2048]{1,0:T(8,128)(2,1)} %get-tuple-element.9.raw_down, bf16[128,2048]{1,0:T(8,128)(2,1)} %get-tuple-element.10.raw_up, f32[1,128]{1,0:T(1,128)} %get-tuple-element.11.raw_slope), custom_call_target="tpu_custom_call" | custom-call | tf_op jit(solution)/shard_map/pallas_call | solution.py:709

commit v6 on v5

--- a/solution.py
+++ b/solution.py
@@ -107,6 +107,8 @@
     back_u,
     slope_row,
     slopes,
+    group_sem,
+    all_sem,
     loc_sem,
     tok_s,
     tok_r,
@@ -144,13 +146,41 @@
     at, ends = payload_rows(layers, half, rank, TILE * layers * ranks)
 
     barrier = pltpu.get_barrier_semaphore()
-    greeted = 0
-    greet = [{axis: peer} for axis in ("tensor", "section", "dp") for peer in peers(axis)]
-    if bits > 1:
-        greet += [{"tensor": tensor ^ 2, "section": peer} for peer in peers("section")]
-    for device in greet:
+    core = tensor & 1
+    sibling = {"tensor": tensor ^ 1}
+
+    def greet(device):
         pl.semaphore_signal(barrier, inc=1, device_id=device, device_id_type=MESH)
-        greeted += 1
+
+    chips = ranks // 2
+    for away in range(layers):
+        for over in range(chips):
+            chip = lax.rem((tensor >> 1) + over, chips)
+            if away or over:
+                greet({"section": lax.rem(section + away, layers), "tensor": 2 * chip + 1})
+    pl.when(core == 0)(lambda: greet(sibling))
+    for peer in peers("dp"):
+        greet({"dp": peer, "tensor": tensor - core})
+
+    def group_arrived():
+        @pl.when(core == 1)
+        def _():
+            pl.semaphore_wait(barrier, layers * ranks - 1)
+            pl.semaphore_signal(group_sem, inc=1, device_id=sibling, device_id_type=MESH)
+
+        @pl.when(core == 0)
+        def _():
+            pl.semaphore_wait(group_sem, 1)
+
+    def all_arrived():
+        @pl.when(core == 0)
+        def _():
+            pl.semaphore_wait(barrier, 2 * (groups - 1))
+            pl.semaphore_signal(all_sem, inc=1, device_id=sibling, device_id_type=MESH)
+
+        @pl.when(core == 1)
+        def _():
+            pl.semaphore_wait(all_sem, 1)
 
     def columns(index):
         return pl.ds(pl.multiple_of(index * fw, LANES), fw)
@@ -177,42 +207,6 @@
     ]
     for load in loads:
         load.start()
-
-    pl.semaphore_wait(barrier, greeted)
-
-    def spread(source, target, send, recv, some=None):
-        def rows_of(ref):
-            return ref if some is None else ref.at[some]
-
-        for peer in peers("section"):
-            pltpu.make_async_remote_copy(
-                rows_of(source).at[:, columns(peer)],
-                rows_of(target.at[section]),
-                send,
-                recv.at[section],
-                {"section": peer},
-                MESH,
-            ).start()
-        pltpu.make_async_copy(
-            rows_of(source).at[:, columns(section)], rows_of(target.at[section]), recv.at[section]
-        ).start()
-
-    for load in loads[5:9]:
-        load.wait()
-    spread(up_v, w_up, wu_s, wu_r)
-    for load in loads[4:5] + loads[9:]:
-        load.wait()
-    down_scaled[...] = (down_v[...].astype(f32) * gains_v[...].astype(f32)).astype(bf16)
-    for part_of in range(2):
-        spread(
-            down_scaled,
-            w_down,
-            wd_s,
-            wd_r.at[part_of],
-            pl.ds(part_of * rank, rank),
-        )
-    gains_wide[...] = jnp.broadcast_to(gains_v[...], gains_wide.shape)
-    spread(gains_wide, w_gain, wg_s, wg_r)
 
     early = lax.broadcasted_iota(jnp.int32, (count, count), 0)
     late = lax.broadcasted_iota(jnp.int32, (count, count), 1)
@@ -243,11 +237,48 @@
         jnp.broadcast_to(flag, (groups * spad, LANES)).astype(bf16).reshape(groups, spad, LANES)
     )
 
+    group_arrived()
+
+    def spread(source, target, send, recv, some=None):
+        def rows_of(ref):
+            return ref if some is None else ref.at[some]
+
+        for peer in peers("section"):
+            pltpu.make_async_remote_copy(
+                rows_of(source).at[:, columns(peer)],
+                rows_of(target.at[section]),
+                send,
+                recv.at[section],
+                {"section": peer},
+                MESH,
+            ).start()
+        pltpu.make_async_copy(
+            rows_of(source).at[:, columns(section)], rows_of(target.at[section]), recv.at[section]
+        ).start()
+
+    for load in loads[5:9]:
+        load.wait()
+    spread(up_v, w_up, wu_s, wu_r)
+    for load in loads[4:5] + loads[9:]:
+        load.wait()
+    down_scaled[...] = (down_v[...].astype(f32) * gains_v[...].astype(f32)).astype(bf16)
+    all_arrived()
     for peer in peers("dp"):
         pltpu.make_async_remote_copy(
             sendbuf.at[peer], recvbuf.at[dp], tok_s, tok_r, {"dp": peer}, MESH
         ).start()
     recvbuf[dp] = sendbuf[dp]
+
+    for part_of in range(2):
+        spread(
+            down_scaled,
+            w_down,
+            wd_s,
+            wd_r.at[part_of],
+            pl.ds(part_of * rank, rank),
+        )
+    gains_wide[...] = jnp.broadcast_to(gains_v[...], gains_wide.shape)
+    spread(gains_wide, w_gain, wg_s, wg_r)
 
     cell = lax.broadcasted_iota(jnp.int32, (1, groups * spad), 1)
     source = sum((cell >= d * spad).astype(jnp.int32) for d in range(1, groups))
@@ -676,6 +707,8 @@
             pltpu.VMEM((layers, weight_rows, fw), b16),
             pltpu.VMEM((8, wide), f32),
             pltpu.VMEM((groups, 8, wide), f32),
+            pltpu.SemaphoreType.REGULAR,
+            pltpu.SemaphoreType.REGULAR,
             dma((13,)),
             dma,
             dma,

time: 100 us -> 98 us (0.980)
  Pallas kernels: 99.6 us -> 97.2 us
    pallas_call x1, Pallas kernels: 97.4 us -> 95.1 us  [on_device(): pl.pallas_call(functools.partial(kernel, cap), out_shape=(jax.ShapeDtypeS...]
where the time goes in v6:
time: 98 us; the launch traced here: 97.9 us
  Pallas kernels  97.2 us (99%)
    pallas_call x1, Pallas kernels, on_device(): pl.pallas_call(functools.partial(kernel, cap), out_shape=(jax.ShapeDtypeS...  95.1 us
    pallas_call x1, Pallas kernels, on_device(): pl.pallas_call(finish, out_shape=tuple((jax.ShapeDtypeStruct(r.shape, r.d...  2.11 us

profile of v6, /device:TPU:1, one launch (start us, length us, event | category | flops | bytes accessed | tf_op | source)
XLA Modules:
  0.0 97.9 jit_solution(3304420213287773186)
XLA Ops:
  0.6 95.1 %shard_map.94 = (bf16[128,2048]{1,0:T(8,128)(2,1)}, bf16[128,2048]{1,0:T(8,128)(2,1)}, f32[1,128]{1,0:T(1,128)}) custom-call(s32[1,128]{1,0:T(1,128)} %bitcast.8, s32[1,128]{1,0:T(1,128)} %bitcast.9, bf16[1,2048]{1,0:T(2,128)(2,1)} %gains.1, bf16[128,2048]{1,0:T(8,128)(2,1)} %bitcast.6, bf16[128,2048]{1,0:T(8,128)(2,1)} %tokens.1, ...), custom_call_target="tpu_custom_call" | custom-call | tf_op jit(solution)/shard_map/pallas_call | solution.py:663
  95.7 2.1 %shard_map.95 = (bf16[128,2048]{1,0:T(8,128)(2,1)}, bf16[128,2048]{1,0:T(8,128)(2,1)}, f32[1,128]{1,0:T(1,128)}) custom-call(bf16[128,2048]{1,0:T(8,128)(2,1)} %get-tuple-element.9.raw_down, bf16[128,2048]{1,0:T(8,128)(2,1)} %get-tuple-element.10.raw_up, f32[1,128]{1,0:T(1,128)} %get-tuple-element.11.raw_slope), custom_call_target="tpu_custom_call" | custom-call | tf_op jit(solution)/shard_map/pallas_call | solution.py:742

commit v7 on v6

--- a/solution.py
+++ b/solution.py
@@ -462,7 +462,7 @@
     advance([0, 1] if bits > 1 else [1])
     down_products(1)
     advance([2])
-    advance([1, 2, 0, 1, 2, 0, 1, 2, 0, 1, 2, 0, 1, 2, 0, 1, 2])
+    advance([1, 0, 2, 0, 1, 2, 0, 1, 2, 0, 1, 2, 0, 1, 2, 0, 1, 2])
 
     def lanes(first, last=None):
         return slice(first * LANES, (first + 1 if last is None else last) * LANES)

time: 98 us -> 95.9 us (0.979)
  Pallas kernels: 97.2 us -> 95.1 us
    pallas_call x1, Pallas kernels: 95.1 us -> 93 us  [on_device(): pl.pallas_call(functools.partial(kernel, cap), out_shape=(jax.ShapeDtypeS...]
where the time goes in v7:
time: 95.9 us; the launch traced here: 95.7 us
  Pallas kernels  95.1 us (99%)
    pallas_call x1, Pallas kernels, on_device(): pl.pallas_call(functools.partial(kernel, cap), out_shape=(jax.ShapeDtypeS...  93 us
    pallas_call x1, Pallas kernels, on_device(): pl.pallas_call(finish, out_shape=tuple((jax.ShapeDtypeStruct(r.shape, r.d...  2.11 us

profile of v7, /device:TPU:1, one launch (start us, length us, event | category | flops | bytes accessed | tf_op | source)
XLA Modules:
  0.0 95.7 jit_solution(6448963347988923626)
XLA Ops:
  0.6 93.0 %shard_map.94 = (bf16[128,2048]{1,0:T(8,128)(2,1)}, bf16[128,2048]{1,0:T(8,128)(2,1)}, f32[1,128]{1,0:T(1,128)}) custom-call(s32[1,128]{1,0:T(1,128)} %bitcast.8, s32[1,128]{1,0:T(1,128)} %bitcast.9, bf16[1,2048]{1,0:T(2,128)(2,1)} %gains.1, bf16[128,2048]{1,0:T(8,128)(2,1)} %bitcast.6, bf16[128,2048]{1,0:T(8,128)(2,1)} %tokens.1, ...), custom_call_target="tpu_custom_call" | custom-call | tf_op jit(solution)/shard_map/pallas_call | solution.py:663
  93.6 2.1 %shard_map.95 = (bf16[128,2048]{1,0:T(8,128)(2,1)}, bf16[128,2048]{1,0:T(8,128)(2,1)}, f32[1,128]{1,0:T(1,128)}) custom-call(bf16[128,2048]{1,0:T(8,128)(2,1)} %get-tuple-element.9.raw_down, bf16[128,2048]{1,0:T(8,128)(2,1)} %get-tuple-element.10.raw_up, f32[1,128]{1,0:T(1,128)} %get-tuple-element.11.raw_slope), custom_call_target="tpu_custom_call" | custom-call | tf_op jit(solution)/shard_map/pallas_call | solution.py:742

commit v8 on v7

--- a/solution.py
+++ b/solution.py
@@ -38,23 +38,41 @@
     return [lax.rem(me + o, count) for o in offsets]
 
 
+def shared_blocks(layers):
+    return (layers - 2, layers - 4) if layers >= 4 else (None, None)
+
+
 def payload_rows(layers, half, rank, unit):
     at, ends = {}, []
     at["squares"], rows = 0, TILE
     for name, count in (("q", layers - 1), ("r", layers)):
         at[name], rows = rows, rows + count * half
-    for k in range(layers - 1):
-        for other in range(k, layers - 1):
-            at["u", k, other], rows = rows, rows + rank
-    rows = round_up(rows, unit)
-    ends.append(rows)
+    blocks = [("u", k, other) for k in range(layers - 1) for other in range(k, layers - 1)]
+    left, right = shared_blocks(layers)
+    later = []
     for part in range(2):
-        at["p", part], rows = rows, rows + layers // 2 * half
+        parts = [(("p", part), layers // 2 * half)]
         for k in range(layers - 1):
             for pair in range((k + 1) // 2, layers // 2):
-                at["m", part, k, pair], rows = rows, rows + rank
+                if k != left:
+                    parts.append((("m", part, k, pair), rank))
+        later.append(parts)
+    free = [-sum(size for _, size in parts) % unit // rank for parts in later]
+    over = -(-((rows + len(blocks) * rank) % unit) // rank)
+    if over <= sum(free):
+        for parts, room in zip(later, free):
+            take = min(room, over)
+            over -= take
+            for _ in range(take):
+                parts.append((blocks.pop(), rank))
+    for parts in [[(block, rank) for block in blocks], *later]:
+        for name, size in parts:
+            at[name], rows = rows, rows + size
         rows = round_up(rows, unit)
         ends.append(rows)
+    for part in range(2):
+        if left is not None:
+            at["m", part, left, layers // 2 - 1] = at["m", part, right, layers // 2 - 2]
     return at, ends
 
 
@@ -144,6 +162,7 @@
     each = slots // groups
     bf16, f32 = jnp.bfloat16, jnp.float32
     at, ends = payload_rows(layers, half, rank, TILE * layers * ranks)
+    left_k, _ = shared_blocks(layers)
 
     barrier = pltpu.get_barrier_semaphore()
     core = tensor & 1
@@ -373,7 +392,12 @@
             for pair in range(skip, layers // 2):
                 row = at["m", h, k, pair]
                 i = pair - skip
-                part[row : row + rank] = thinned(product[:, i * LANES : (i + 1) * LANES])
+                block = thinned(product[:, i * LANES : (i + 1) * LANES])
+                if k == left_k:
+                    block = jnp.where(
+                        left_rank, pltpu.roll(block.astype(f32), rank, 1), part[row : row + rank]
+                    ).astype(bf16)
+                part[row : row + rank] = block
 
     def rows(first, size):
         return pl.ds(pl.multiple_of(first, TILE), size)
@@ -488,7 +512,7 @@
             )
             for which in range(2):
                 if 2 * pair + which > k:
-                    block = layer_of(first, last, which, left_rank)
+                    block = layer_of(first, last, 0 if k == left_k else which, left_rank)
                     big_m[k, :, lanes(2 * pair + which)] = widened(block)
     folded = fin[0:TILE].astype(f32)
     squares = jnp.concatenate(

time: 95.9 us -> 93.7 us (0.977)
  Pallas kernels: 95.1 us -> 92.9 us
    pallas_call x1, Pallas kernels: 93 us -> 90.8 us  [on_device(): pl.pallas_call(functools.partial(kernel, cap), out_shape=(jax.ShapeDtypeS...]
where the time goes in v8:
time: 93.7 us; the launch traced here: 93.6 us
  Pallas kernels  92.9 us (99%)
    pallas_call x1, Pallas kernels, on_device(): pl.pallas_call(functools.partial(kernel, cap), out_shape=(jax.ShapeDtypeS...  90.8 us
    pallas_call x1, Pallas kernels, on_device(): pl.pallas_call(finish, out_shape=tuple((jax.ShapeDtypeStruct(r.shape, r.d...  2.11 us

profile of v8, /device:TPU:1, one launch (start us, length us, event | category | flops | bytes accessed | tf_op | source)
XLA Modules:
  0.0 93.6 jit_solution(15404303783845250719)
XLA Ops:
  0.6 90.8 %shard_map.94 = (bf16[128,2048]{1,0:T(8,128)(2,1)}, bf16[128,2048]{1,0:T(8,128)(2,1)}, f32[1,128]{1,0:T(1,128)}) custom-call(s32[1,128]{1,0:T(1,128)} %bitcast.8, s32[1,128]{1,0:T(1,128)} %bitcast.9, bf16[1,2048]{1,0:T(2,128)(2,1)} %gains.1, bf16[128,2048]{1,0:T(8,128)(2,1)} %bitcast.6, bf16[128,2048]{1,0:T(8,128)(2,1)} %tokens.1, ...), custom_call_target="tpu_custom_call" | custom-call | tf_op jit(solution)/shard_map/pallas_call | solution.py:687
  91.5 2.1 %shard_map.95 = (bf16[128,2048]{1,0:T(8,128)(2,1)}, bf16[128,2048]{1,0:T(8,128)(2,1)}, f32[1,128]{1,0:T(1,128)}) custom-call(bf16[128,2048]{1,0:T(8,128)(2,1)} %get-tuple-element.9.raw_down, bf16[128,2048]{1,0:T(8,128)(2,1)} %get-tuple-element.10.raw_up, f32[1,128]{1,0:T(1,128)} %get-tuple-element.11.raw_slope), custom_call_target="tpu_custom_call" | custom-call | tf_op jit(solution)/shard_map/pallas_call | solution.py:766

commit v9 on v8

--- a/solution.py
+++ b/solution.py
@@ -486,7 +486,7 @@
     advance([0, 1] if bits > 1 else [1])
     down_products(1)
     advance([2])
-    advance([1, 0, 2, 0, 1, 2, 0, 1, 2, 0, 1, 2, 0, 1, 2, 0, 1, 2])
+    advance([1, 0, 2, 0, 1, 0, 2, 1, 2, 0, 1, 2, 0, 1, 2, 0, 1, 2])
 
     def lanes(first, last=None):
         return slice(first * LANES, (first + 1 if last is None else last) * LANES)
@@ -582,8 +582,8 @@
         back_u[layer] = (SCALE * matmul(zs[layer], gs[layer], TN)).astype(bf16)
         return back_u.at[layer], grad_up.at[:, columns(section)], gu_s, gu_r
 
-    for make in (down_grad, up_grad):
-        for layer in peers("section"):
+    for layer in peers("section"):
+        for make in (down_grad, up_grad):
             source, target, send, recv = make(layer)
             pltpu.make_async_remote_copy(
                 source, target, send, recv, {"section": layer}, MESH

time: 93.7 us -> 94.3 us (level)
  no operation moved by 1% of the time
where the time goes in v9:
time: 94.3 us; the launch traced here: 94.2 us
  Pallas kernels  93.5 us (99%)
    pallas_call x1, Pallas kernels, on_device(): pl.pallas_call(functools.partial(kernel, cap), out_shape=(jax.ShapeDtypeS...  91.4 us
    pallas_call x1, Pallas kernels, on_device(): pl.pallas_call(finish, out_shape=tuple((jax.ShapeDtypeStruct(r.shape, r.d...  2.11 us

profile of v9, /device:TPU:1, one launch (start us, length us, event | category | flops | bytes accessed | tf_op | source)
XLA Modules:
  0.0 94.2 jit_solution(5092428836113781354)
XLA Ops:
  0.6 91.4 %shard_map.94 = (bf16[128,2048]{1,0:T(8,128)(2,1)}, bf16[128,2048]{1,0:T(8,128)(2,1)}, f32[1,128]{1,0:T(1,128)}) custom-call(s32[1,128]{1,0:T(1,128)} %bitcast.8, s32[1,128]{1,0:T(1,128)} %bitcast.9, bf16[1,2048]{1,0:T(2,128)(2,1)} %gains.1, bf16[128,2048]{1,0:T(8,128)(2,1)} %bitcast.6, bf16[128,2048]{1,0:T(8,128)(2,1)} %tokens.1, ...), custom_call_target="tpu_custom_call" | custom-call | tf_op jit(solution)/shard_map/pallas_call | solution.py:687
  92.0 2.1 %shard_map.95 = (bf16[128,2048]{1,0:T(8,128)(2,1)}, bf16[128,2048]{1,0:T(8,128)(2,1)}, f32[1,128]{1,0:T(1,128)}) custom-call(bf16[128,2048]{1,0:T(8,128)(2,1)} %get-tuple-element.9.raw_down, bf16[128,2048]{1,0:T(8,128)(2,1)} %get-tuple-element.10.raw_up, f32[1,128]{1,0:T(1,128)} %get-tuple-element.11.raw_slope), custom_call_target="tpu_custom_call" | custom-call | tf_op jit(solution)/shard_map/pallas_call | solution.py:766
